TPU v7x, 32 devices: a whole 2x2x4 slice. The times are simulated.
32 devices in a mesh: dom: 16 (over z, y, core), tile: 2 (over x).
Axes of the slice: x: 2, y: 2, z: 4, core: 2. Of those that a mesh axis runs over, the one named last changes fastest.
Arguments:
- states: float32 [16, 3, 128, 2048], P('dom', None, 'tile'), may hold values from -6 to 6
- offspring: int32 [16], replicated, may hold values from 0 to 4, as said below
- sea_depth: float32 [128, 2048], P('tile'), may hold values from 0.5 to 2
- wind: bfloat16 [6, 2, 64, 1024], P('tile'), may hold values from -6 to 6
- start_hour: int32 [1], replicated, may hold values from 0 to 4
Outputs:
- new_states: float32 [16, 3, 128, 2048], P('dom', None, 'tile')
Inputs may be any that keep to these rules, and one draw needn't show every extreme that they name: offspring counts are whole numbers that sum to 16. The step runs from hour start_hour[0] to the next hour.
All inputs are finite; a program needn't handle non-finite values.
Results may differ from a plain program's by a relative error of at most 0.001.
Values may be sent and summed in bfloat16 or wider, within the bound.
No kernel may reach another device: no remote copies, remote signals or barrier semaphores. Data moves between devices by JAX's collectives and lax.ppermute only.
A program may use at most 128 MiB of HBM per device.

v0:
```python
import jax
import jax.numpy as jnp
from jax import lax
from jax.sharding import PartitionSpec as P

GRAVITY = 1.0
FRICTION = 0.1
TIME_STEP = 0.4


def from_root(value, axis, root):
    mine = lax.axis_index(axis) == root
    return lax.psum(jnp.where(mine, value, jnp.zeros_like(value)), axis)


def for_sending(value):

    def short(part):
        return part.astype(jnp.bfloat16) if part.dtype == jnp.float32 else part

    return jax.tree.map(short, value)


def with_halo(cells, sides, width):
    for axis, dim in sides:
        count = lax.axis_size(axis)
        ends = count - 1
        head = lax.slice_in_dim(cells, 0, width, axis=dim)
        tail = lax.slice_in_dim(cells, cells.shape[dim] - width, cells.shape[dim], axis=dim)
        cells = jnp.concatenate(
            [
                lax.ppermute(tail, axis, [(i, (i + 1) % count) for i in range(ends)]),
                cells,
                lax.ppermute(head, axis, [((i + 1) % count, i) for i in range(ends)]),
            ],
            axis=dim,
        )
    return cells


def parent_list(offspring):
    count = offspring.shape[0]
    running = jnp.cumsum(offspring)
    slots = jnp.arange(count, dtype=jnp.int32)
    return jnp.sum((running[None, :] <= slots[:, None]).astype(jnp.int32), axis=1)


def along_cols(field):
    return (jnp.roll(field, -1, axis=-1) - jnp.roll(field, 1, axis=-1)) * 0.5


def along_rows(padded):
    return (padded[..., 2:, :] - padded[..., :-2, :]) * 0.5


def upsample(panel):
    return jnp.repeat(jnp.repeat(panel, 2, axis=-2), 2, axis=-1).astype(jnp.float32)


def spin_rate(global_rows, total_rows):
    return (0.1 + 0.4 * global_rows.astype(jnp.float32) / total_rows)[:, None]


def body(states, offspring, sea_depth, wind, start_hour):
    part_dev = states.shape[0]
    row_count = states.shape[2]
    dom_size = lax.axis_size("dom")
    tile_size = lax.axis_size("tile")
    total_rows = row_count * tile_size
    parents = parent_list(offspring)
    spread = lax.all_to_all(
        states.reshape(part_dev, dom_size, -1), "dom", split_axis=1, concat_axis=0, tiled=True
    )
    picked = jnp.take(spread, parents, axis=0)
    copied = lax.all_to_all(picked, "dom", split_axis=0, concat_axis=1, tiled=True).reshape(
        states.shape
    )
    hours_dev = wind.shape[0]
    first = start_hour[0]
    second = first + 1
    half_rows = row_count // 2
    coarse_start = lax.axis_index("tile") * half_rows

    def hour_panel(hour):
        local = lax.dynamic_index_in_dim(wind, hour % hours_dev, 0, keepdims=False)
        whole = from_root(local, "tile", hour // hours_dev)
        return lax.dynamic_slice_in_dim(whole, coarse_start, half_rows, 1)

    wind_now = upsample(hour_panel(first))
    wind_next = upsample(hour_panel(second))
    row_start = lax.axis_index("tile") * row_count
    wind_mid = 0.5 * (wind_now + wind_next)
    spin = spin_rate(row_start + jnp.arange(row_count, dtype=jnp.int32), total_rows)

    def rate(state, stress):
        surface = state[:, 0]
        eastward = state[:, 1]
        northward = state[:, 2]
        flux_east = sea_depth * eastward
        flux_north = sea_depth * northward
        rims = with_halo(for_sending(jnp.stack([surface, flux_north], axis=1)), (("tile", 2),), 1)
        d_surface = -(along_cols(flux_east) + along_rows(rims[:, 1]))
        d_east = spin * northward - GRAVITY * along_cols(surface) + stress[0] - FRICTION * eastward
        d_north = (
            -spin * eastward - GRAVITY * along_rows(rims[:, 0]) + stress[1] - FRICTION * northward
        )
        return jnp.stack([d_surface, d_east, d_north], axis=1)

    section_one = copied + TIME_STEP * rate(copied, wind_now)
    section_two = 0.75 * copied + 0.25 * (section_one + TIME_STEP * rate(section_one, wind_next))
    result = 1.0 / 3.0 * copied + 2.0 / 3.0 * (
        section_two + TIME_STEP * rate(section_two, wind_mid)
    )
    return result


def solution(mesh):
    return jax.shard_map(
        body,
        mesh=mesh,
        in_specs=(
            P("dom", None, "tile", None),
            P(),
            P("tile", None),
            P("tile", None, None, None),
            P(),
        ),
        out_specs=P("dom", None, "tile", None),
        check_vma=False,
    )
```

profile of v0, /device:TPU:0, one launch (start us, length us, event | category | flops | bytes accessed | tf_op | source)
XLA Modules:
  0.0 162.9 jit_solution(17294090334004589410)
XLA Ops:
  6.5 3.9 %reshape.1147 = f32[1,16,24576]{2,0,1:T(1,128)} reshape(f32[1,3,64,2048]{3,2,1,0:T(8,128)} %param.5) | data formatting | bytes 3145728 | tf_op jit(solution)/shard_map/reshape | solution.py:72
  10.5 7.5 %all-to-all-start = ((f32[1,16,24576]{2,0,1:T(1,128)}), f32[1,16,24576]{2,0,1:T(1,128)S(1)}, u32[]{:S(2)}, u32[]{:S(2)}) async-start(f32[1,16,24576]{2,0,1:T(1,128)} %reshape.1147), calls=%async_computation | async-start | bytes 3145728 | tf_op jit(solution)/shard_map/all_to_all | solution.py:71
  18.4 31.6 %all-to-all-done = f32[1,16,24576]{2,0,1:T(1,128)S(1)} async-done(((f32[1,16,24576]{2,0,1:T(1,128)}), f32[1,16,24576]{2,0,1:T(1,128)S(1)}, u32[]{:S(2)}, u32[]{:S(2)}) %all-to-all-start) | async-done | bytes 1572896 | tf_op jit(solution)/shard_map/all_to_all | solution.py:71
  52.2 2.8 %copy.101 = f32[16,1,24576]{2,1,0:T(1,128)} copy(f32[16,1,24576]{2,0,1:T(8,128)S(1)} %bitcast_select_fusion) | data formatting | bytes 3145728 | tf_op jit(solution)/shard_map/jit(_take)/select_n | solution.py:74
  54.9 9.2 %all-to-all-start.1 = ((f32[16,1,24576]{2,1,0:T(1,128)}), f32[16,1,24576]{2,1,0:T(1,128)S(1)}, u32[]{:S(2)}, u32[]{:S(2)}) async-start(f32[16,1,24576]{2,1,0:T(1,128)} %copy.101), calls=%async_computation.1 | async-start | bytes 3145728 | tf_op jit(solution)/shard_map/all_to_all | solution.py:75
  66.0 31.5 %all-reduce.3.cloned.1.call-done = (bf16[2,64,1024]{2,1,0:T(8,128)(2,1)}, bf16[2,64,1024]{2,1,0:T(8,128)(2,1)}) async-done(((bf16[2,64,1024]{2,1,0:T(8,128)(2,1)}, bf16[2,64,1024]{2,1,0:T(8,128)(2,1)}), (bf16[2,64,1024]{2,1,0:T(8,128)(2,1)}, bf16[2,64,1024]{2,1,0:T(8,128)(2,1)})) %all-reduce.3.cloned.1.call-update) | async-done | bytes 524304 | tf_op jit(solution)/shard_map/psum | solution.py:13
  105.7 1.4 broadcast_in_dim.55
  107.1 1.1 copy.109
  108.2 1.4 broadcast_in_dim.53
  109.6 1.1 copy.107
  110.7 1.4 broadcast_in_dim.59
  112.1 1.1 copy.117
  113.3 1.4 broadcast_in_dim.63
  114.7 1.1 copy.125
  115.8 1.4 broadcast_in_dim.61
  118.6 1.1 copy.115
  119.8 3.8 %reduce.1 = f32[16,24576]{1,0:T(8,128)S(1)} reduce(f32[16,1,24576]{2,1,0:T(1,128)S(1)} %all-to-all-done.1, f32[]{:T(128)} %constant.94), dimensions={1}, to_apply=%all_to_all.8.reduce_sub_computation | reduce | bytes 3145732 | tf_op jit(solution)/shard_map/all_to_all | solution.py:75
  125.3 1.3 collective-permute-start.1
  126.6 4.8 %collective-permute-start = (bf16[1,2,1,2048]{3,1,2,0:T(2,128)(2,1)S(1)}, bf16[1,2,1,2048]{3,1,2,0:T(2,128)(2,1)S(1)}, u32[]{:S(2)}, u32[]{:S(2)}) collective-permute-start(bf16[1,2,1,2048]{3,1,2,0:T(2,128)(2,1)S(1)} %copy.102), channel_id=1, source_target_pairs={{0,1},{2,3},{4,5},{6,7},{8,9},{10,11},{12,13},{14,15},{16,17},{18,... | collective-permute-start | bytes 24584 | tf_op jit(solution)/shard_map/ppermute | solution.py:32
  135.1 1.3 collective-permute-start.3
  136.4 4.5 %collective-permute-start.2 = (bf16[1,2,1,2048]{3,1,2,0:T(2,128)(2,1)S(1)}, bf16[1,2,1,2048]{3,1,2,0:T(2,128)(2,1)S(1)}, u32[]{:S(2)}, u32[]{:S(2)}) collective-permute-start(bf16[1,2,1,2048]{3,1,2,0:T(2,128)(2,1)S(1)} %copy.110), channel_id=1, source_target_pairs={{0,1},{2,3},{4,5},{6,7},{8,9},{10,11},{12,13},{14,15},{16,17},{18,... | collective-permute-start | bytes 24584 | tf_op jit(solution)/shard_map/ppermute | solution.py:32
  145.1 1.3 collective-permute-start.5
  146.4 4.5 %collective-permute-start.4 = (bf16[1,2,1,2048]{3,1,2,0:T(2,128)(2,1)S(1)}, bf16[1,2,1,2048]{3,1,2,0:T(2,128)(2,1)S(1)}, u32[]{:S(2)}, u32[]{:S(2)}) collective-permute-start(bf16[1,2,1,2048]{3,1,2,0:T(2,128)(2,1)S(1)} %copy.118), channel_id=1, source_target_pairs={{0,1},{2,3},{4,5},{6,7},{8,9},{10,11},{12,13},{14,15},{16,17},{18,... | collective-permute-start | bytes 24584 | tf_op jit(solution)/shard_map/ppermute | solution.py:32
  154.2 1.9 %fusion.6 = f32[1,3,64,2048]{3,2,1,0:T(8,128)} fusion(f32[1,1,64,2048]{3,2,1,0:T(8,128)S(1)} %get-tuple-element.14, f32[1,1,64,2048]{3,2,1,0:T(8,128)S(1)} %get-tuple-element.13, f32[1,1,64,2048]{3,2,1,0:T(8,128)S(1)} %fusion.28, f32[1,3,64,2048]{3,2,1,0:T(8,128)S(1)} %reshape.1148, f32[1,1,64,2048]{3,2,1,0:T(8,128)S(1)} %get-tuple-element.16, ...), kind=kLoop, calls=%fused_computation.10 | loop fusion | flops 7077888 | bytes 7864320 | tf_op jit(solution)/shard_map/add | solution.py:111
  (119 shorter events, 25.7 us)
Async XLA Ops:
  10.5 7.5 %copy-start.10 = (s32[16]{0:T(128)S(1)}, s32[16]{0:T(128)}, u32[]{:S(2)}) copy-start(s32[16]{0:T(128)} %param.6) | copy-start | bytes 196
  10.5 39.5 %all-to-all-start = ((f32[1,16,24576]{2,0,1:T(1,128)}), f32[1,16,24576]{2,0,1:T(1,128)S(1)}, u32[]{:S(2)}, u32[]{:S(2)}) async-start(f32[1,16,24576]{2,0,1:T(1,128)} %reshape.1147), calls=%async_computation | async-start | bytes 3145728 | tf_op jit(solution)/shard_map/all_to_all | solution.py:71
  54.9 10.2 %copy-start.7 = (bf16[3,2,64,1024]{3,2,1,0:T(8,128)(2,1)S(1)}, bf16[3,2,64,1024]{3,2,1,0:T(8,128)(2,1)}, u32[]{:S(2)}) copy-start(bf16[3,2,64,1024]{3,2,1,0:T(8,128)(2,1)} %param.8) | copy-start | bytes 2359300
  54.9 64.8 %all-to-all-start.1 = ((f32[16,1,24576]{2,1,0:T(1,128)}), f32[16,1,24576]{2,1,0:T(1,128)S(1)}, u32[]{:S(2)}, u32[]{:S(2)}) async-start(f32[16,1,24576]{2,1,0:T(1,128)} %copy.101), calls=%async_computation.1 | async-start | bytes 3145728 | tf_op jit(solution)/shard_map/all_to_all | solution.py:75
  64.2 33.3 %all-reduce.3.cloned.1.call-start = ((), (), s32[]{:S(2)}) async-start(), calls=%async_computation.2 | async-start | bytes 1048576 | tf_op jit(solution)/shard_map/psum | solution.py:13
  97.5 1.4 copy-start.8
  97.5 1.4 copy-start.9
  124.0 1.0 copy-start
  125.3 6.4 %collective-permute-start.1 = (bf16[1,2,1,2048]{3,1,2,0:T(2,128)(2,1)S(1)}, bf16[1,2,1,2048]{3,1,2,0:T(2,128)(2,1)S(1)}, u32[]{:S(2)}, u32[]{:S(2)}) collective-permute-start(bf16[1,2,1,2048]{3,1,2,0:T(2,128)(2,1)S(1)} %copy.103), channel_id=1, source_target_pairs={{1,0},{3,2},{5,4},{7,6},{9,8},{11,10},{13,12},{15,14},{17,16},{19,... | collective-permute-start | bytes 24584 | tf_op jit(solution)/shard_map/ppermute | solution.py:34
  126.6 5.9 %collective-permute-start = (bf16[1,2,1,2048]{3,1,2,0:T(2,128)(2,1)S(1)}, bf16[1,2,1,2048]{3,1,2,0:T(2,128)(2,1)S(1)}, u32[]{:S(2)}, u32[]{:S(2)}) collective-permute-start(bf16[1,2,1,2048]{3,1,2,0:T(2,128)(2,1)S(1)} %copy.102), channel_id=1, source_target_pairs={{0,1},{2,3},{4,5},{6,7},{8,9},{10,11},{12,13},{14,15},{16,17},{18,... | collective-permute-start | bytes 24584 | tf_op jit(solution)/shard_map/ppermute | solution.py:32
  132.7 1.0 copy-start.5
  132.7 1.2 copy-start.6
  135.1 6.1 %collective-permute-start.3 = (bf16[1,2,1,2048]{3,1,2,0:T(2,128)(2,1)S(1)}, bf16[1,2,1,2048]{3,1,2,0:T(2,128)(2,1)S(1)}, u32[]{:S(2)}, u32[]{:S(2)}) collective-permute-start(bf16[1,2,1,2048]{3,1,2,0:T(2,128)(2,1)S(1)} %copy.111), channel_id=1, source_target_pairs={{1,0},{3,2},{5,4},{7,6},{9,8},{11,10},{13,12},{15,14},{17,16},{19,... | collective-permute-start | bytes 24584 | tf_op jit(solution)/shard_map/ppermute | solution.py:34
  136.4 5.9 %collective-permute-start.2 = (bf16[1,2,1,2048]{3,1,2,0:T(2,128)(2,1)S(1)}, bf16[1,2,1,2048]{3,1,2,0:T(2,128)(2,1)S(1)}, u32[]{:S(2)}, u32[]{:S(2)}) collective-permute-start(bf16[1,2,1,2048]{3,1,2,0:T(2,128)(2,1)S(1)} %copy.110), channel_id=1, source_target_pairs={{0,1},{2,3},{4,5},{6,7},{8,9},{10,11},{12,13},{14,15},{16,17},{18,... | collective-permute-start | bytes 24584 | tf_op jit(solution)/shard_map/ppermute | solution.py:32
  142.5 1.0 copy-start.3
  142.5 1.2 copy-start.4
  145.1 6.1 %collective-permute-start.5 = (bf16[1,2,1,2048]{3,1,2,0:T(2,128)(2,1)S(1)}, bf16[1,2,1,2048]{3,1,2,0:T(2,128)(2,1)S(1)}, u32[]{:S(2)}, u32[]{:S(2)}) collective-permute-start(bf16[1,2,1,2048]{3,1,2,0:T(2,128)(2,1)S(1)} %copy.119), channel_id=1, source_target_pairs={{1,0},{3,2},{5,4},{7,6},{9,8},{11,10},{13,12},{15,14},{17,16},{19,... | collective-permute-start | bytes 24584 | tf_op jit(solution)/shard_map/ppermute | solution.py:34
  146.4 5.9 %collective-permute-start.4 = (bf16[1,2,1,2048]{3,1,2,0:T(2,128)(2,1)S(1)}, bf16[1,2,1,2048]{3,1,2,0:T(2,128)(2,1)S(1)}, u32[]{:S(2)}, u32[]{:S(2)}) collective-permute-start(bf16[1,2,1,2048]{3,1,2,0:T(2,128)(2,1)S(1)} %copy.118), channel_id=1, source_target_pairs={{0,1},{2,3},{4,5},{6,7},{8,9},{10,11},{12,13},{14,15},{16,17},{18,... | collective-permute-start | bytes 24584 | tf_op jit(solution)/shard_map/ppermute | solution.py:32
  152.5 1.0 copy-start.1
  152.5 1.2 copy-start.2
Sparse Core Ops, SparseCore 0:
  67.4 30.0 all-reduce.2
where the time goes:
time: 164 us; the launch traced here: 163 us
  waiting for transfers between devices  66 us (40%)
  local copies, waits for them, and re-layouts  35.8 us (22%)
  starting transfers between devices  34.7 us (21%)
  between operations  14.7 us (9%)
  other arithmetic  11.8 us (7%)
    all_to_all x1, waiting for transfers between devices, body(): lax.all_to_all(states.reshape(part_dev, dom_size, -1), 'dom', split_axis=...  31.6 us
    psum x1, waiting for transfers between devices, from_root(): return lax.psum(jnp.where(mine, value, jnp.zeros_like(value)), axis)  31.5 us
    ppermute x3, starting transfers between devices, with_halo(): lax.ppermute(tail, axis, [(i, (i + 1) % count) for i in range(ends)])  13.8 us
    all_to_all x1, starting transfers between devices, body(): lax.all_to_all(picked, 'dom', split_axis=0, concat_axis=1, tiled=True)  9.24 us
    all_to_all x1, starting transfers between devices, body(): lax.all_to_all(states.reshape(part_dev, dom_size, -1), 'dom', split_axis=...  7.52 us
    broadcast_in_dim x6, local copies, waits for them, and re-layouts, upsample(): jnp.repeat(jnp.repeat(panel, 2, axis=-2), 2, axis=-1).astype(jnp.float32)  7.37 us
    slice x9, local copies, waits for them, and re-layouts, rate(): stress[1]  6.94 us
    slice x12, local copies, waits for them, and re-layouts, rate(): stress[0]  6.14 us
  transfers between devices with their start and end apart: 9, of which 5 were waited for; matrix products, arithmetic and copies ran while one was open for 15% of the time, Pallas kernels for 0%

commit v1 on v0

v1 whole, which is shorter than its diff:
```python
import functools

import jax
import jax.numpy as jnp
from jax import lax
from jax.experimental import pallas as pl
from jax.experimental.pallas import tpu as pltpu
from jax.sharding import PartitionSpec as P

FRICTION = 0.1
TIME_STEP = 0.4
EDGE = 3
PAD = 8
VMEM_BYTES = 48 * 1024 * 1024


def parent_list(offspring):
    count = offspring.shape[0]
    running = jnp.cumsum(offspring)
    slots = jnp.arange(count, dtype=jnp.int32)
    return jnp.sum((running[None, :] <= slots[:, None]).astype(jnp.int32), axis=1)


def swap_edges(head, tail):
    count = lax.axis_size("tile")
    me = lax.axis_index("tile")
    above = jnp.zeros_like(head)
    below = jnp.zeros_like(head)
    for parity in range(2):
        pairs = []
        for i in range(parity, count - 1, 2):
            pairs += [(i, i + 1), (i + 1, i)]
        if pairs:
            upper = me % 2 == parity
            got = lax.ppermute(jnp.where(upper, tail, head), "tile", pairs)
            below = jnp.where(upper, got, below)
            above = jnp.where(upper, above, got)
    return above, below


def wind_window(wind, start_hour, row_count):
    count = lax.axis_size("tile")
    me = lax.axis_index("tile")
    hours_dev, parts, coarse_rows, coarse_cols = wind.shape
    own_rows = row_count // 2
    window = min(own_rows + 2 * PAD, coarse_rows)

    def first_row(tile):
        return jnp.clip(tile * own_rows - PAD, 0, coarse_rows - window)

    hours = [start_hour[0], start_hour[0] + 1]

    def panels(tile):
        return jnp.concatenate(
            [
                lax.dynamic_slice(
                    wind, (hour % hours_dev, 0, first_row(tile), 0), (1, parts, window, coarse_cols)
                )
                for hour in hours
            ]
        )

    owner = jnp.stack(hours)[:, None, None, None] // hours_dev
    found = panels(me)
    for shift in range(1, count):
        got = lax.ppermute(
            panels((me + shift) % count), "tile", [(i, (i + shift) % count) for i in range(count)]
        )
        found = jnp.where(owner == (me - shift) % count, got, found)
    return found, first_row(me)


def wind_kernel(where_ref, coarse_ref, fine_ref):
    hours, parts, window, coarse_cols = coarse_ref.shape
    rows = fine_ref.shape[2]
    first = where_ref[0]
    base = where_ref[1]
    fine_row = lax.broadcasted_iota(jnp.int32, (rows, window), 0) + first
    coarse_row = lax.broadcasted_iota(jnp.int32, (rows, window), 1) + base
    lift = jnp.where((fine_row >> 1) == coarse_row, 1.0, 0.0).astype(jnp.bfloat16)
    step = 128
    fine_col = lax.broadcasted_iota(jnp.int32, (step, 2 * step), 1)
    coarse_col = lax.broadcasted_iota(jnp.int32, (step, 2 * step), 0)
    widen = jnp.where((fine_col >> 1) == coarse_col, 1.0, 0.0).astype(jnp.bfloat16)
    for hour in range(hours):
        for part in range(parts):
            for left in range(0, coarse_cols, step):
                cells = coarse_ref[hour, part, :, left : left + step]
                wide = jnp.dot(cells, widen, preferred_element_type=jnp.float32)
                tall = jnp.dot(
                    lift, wide.astype(jnp.bfloat16), preferred_element_type=jnp.float32
                )
                fine_ref[hour, part, :, 2 * left : 2 * (left + step)] = TIME_STEP * tall


def fine_wind(coarse, first, base, rows):
    hours, parts, window, cols = coarse.shape
    return pl.pallas_call(
        wind_kernel,
        out_shape=jax.ShapeDtypeStruct((hours, parts, rows, 2 * cols), jnp.float32),
        in_specs=[
            pl.BlockSpec(memory_space=pltpu.SMEM),
            pl.BlockSpec(memory_space=pltpu.VMEM),
        ],
        out_specs=pl.BlockSpec(memory_space=pltpu.VMEM),
        compiler_params=pltpu.CompilerParams(vmem_limit_bytes=VMEM_BYTES),
        cost_estimate=pl.CostEstimate(
            flops=4 * hours * parts * rows * window * cols,
            bytes_accessed=8 * hours * parts * rows * cols,
            transcendentals=0,
        ),
    )(jnp.stack([first, base]).astype(jnp.int32), coarse)


def step_kernel(total_rows, where_ref, state_ref, depth_ref, wind_ref, out_ref, one, two, flux):
    rows = state_ref.shape[1]
    cols = state_ref.shape[2]
    blocks = rows // PAD
    first = where_ref[0]

    def shifted(ref, index, row, by):
        if 0 <= row + by <= rows - PAD:
            return ref[index, row + by : row + by + PAD, :]
        return pltpu.roll(ref[index, row : row + PAD, :], -by % PAD, 0)

    def across(field):
        return pltpu.roll(field, cols - 1, 1) - pltpu.roll(field, 1, 1)

    def section(source, stress, share, store, chosen):
        for block in range(blocks):
            low = block * PAD
            here = pl.ds(low, PAD)
            flux[0, here, :] = depth_ref[here, :] * source[2, here, :]
        for block in chosen:
            low = block * PAD
            here = pl.ds(low, PAD)
            row = first + low + lax.broadcasted_iota(jnp.int32, (PAD, 1), 0)
            turn = TIME_STEP * (0.1 + 0.4 * row.astype(jnp.float32) / total_rows)
            surface = source[0, here, :]
            east = source[1, here, :]
            north = source[2, here, :]
            flux_up = shifted(flux, 0, low, 1) - shifted(flux, 0, low, -1)
            next_surface = surface - (across(depth_ref[here, :] * east) + flux_up)
            rise = shifted(source, 0, low, 1) - shifted(source, 0, low, -1)
            half = 0.5 * TIME_STEP
            keep = 1.0 - TIME_STEP * FRICTION
            next_east = keep * east + turn * north - half * across(surface) + stress(0, here)
            next_north = keep * north - turn * east - half * rise + stress(1, here)
            inside = None
            if block == 0 or block == blocks - 1:
                inside = (row >= 0) & (row < total_rows)
            for part, value in enumerate((next_surface, next_east, next_north)):
                if share != 1.0:
                    value = (1.0 - share) * state_ref[part, here, :] + share * value
                if inside is not None:
                    value = jnp.where(inside, value, 0.0)
                store(part, low, value)

    def into(target):
        def store(part, low, value):
            target[part, pl.ds(low, PAD), :] = value

        return store

    def finish(part, low, value):
        out_ref[part, pl.ds(low - PAD, PAD), :] = value

    everything = range(blocks)
    section(state_ref, lambda part, here: wind_ref[0, part, here, :], 1.0, into(one), everything)
    section(one, lambda part, here: wind_ref[1, part, here, :], 0.25, into(two), everything)
    section(
        two,
        lambda part, here: 0.5 * (wind_ref[0, part, here, :] + wind_ref[1, part, here, :]),
        2.0 / 3.0,
        finish,
        range(1, blocks - 1),
    )


def step(state, depth, wind, first, total_rows):
    parts, rows, cols = state.shape
    own = rows - 2 * PAD
    vmem = pl.BlockSpec(memory_space=pltpu.VMEM)
    return pl.pallas_call(
        functools.partial(step_kernel, total_rows),
        out_shape=jax.ShapeDtypeStruct((parts, own, cols), jnp.float32),
        in_specs=[pl.BlockSpec(memory_space=pltpu.SMEM), vmem, vmem, vmem],
        out_specs=vmem,
        scratch_shapes=[
            pltpu.VMEM((parts, rows, cols), jnp.float32),
            pltpu.VMEM((parts, rows, cols), jnp.float32),
            pltpu.VMEM((1, rows, cols), jnp.float32),
        ],
        compiler_params=pltpu.CompilerParams(vmem_limit_bytes=VMEM_BYTES),
        cost_estimate=pl.CostEstimate(
            flops=100 * parts * rows * cols,
            bytes_accessed=4 * (3 * parts + 3) * rows * cols,
            transcendentals=0,
        ),
    )(first[None].astype(jnp.int32), state, depth, wind)


def exchange_all(cells, parents):
    spread = lax.all_to_all(cells, "dom", split_axis=3, concat_axis=0, tiled=True)
    picked = jnp.take(spread, parents, axis=0)
    return lax.all_to_all(picked, "dom", split_axis=0, concat_axis=3, tiled=True)


def body(states, offspring, sea_depth, wind, start_hour):
    row_count = states.shape[2]
    total_rows = row_count * lax.axis_size("tile")
    first = lax.axis_index("tile") * row_count - PAD
    parents = parent_list(offspring)
    coarse, base = wind_window(wind, start_hour, row_count)
    rows = row_count + 2 * PAD
    stress = fine_wind(coarse, first, base, rows)
    fill = ((PAD - EDGE, 0), (0, 0)), ((0, PAD - EDGE), (0, 0))

    depth_above, depth_below = swap_edges(sea_depth[:EDGE], sea_depth[-EDGE:])
    depth = (0.5 * TIME_STEP) * jnp.concatenate(
        [jnp.pad(depth_above, fill[0]), sea_depth, jnp.pad(depth_below, fill[1])]
    )
    copied = exchange_all(states.astype(jnp.float16), parents)[0]
    above, below = swap_edges(copied[:, :EDGE], copied[:, -EDGE:])
    state = jnp.concatenate(
        [
            jnp.pad(above, ((0, 0),) + fill[0]),
            copied,
            jnp.pad(below, ((0, 0),) + fill[1]),
        ],
        axis=1,
    ).astype(jnp.float32)
    return step(state, depth, stress, first, total_rows)[None]


def solution(mesh):
    return jax.shard_map(
        body,
        mesh=mesh,
        in_specs=(
            P("dom", None, "tile", None),
            P(),
            P("tile", None),
            P("tile", None, None, None),
            P(),
        ),
        out_specs=P("dom", None, "tile", None),
        check_vma=False,
    )
```

time: 164 us -> 74.3 us (0.45)
  waiting for transfers between devices: 66 us -> 33.6 us
  local copies, waits for them, and re-layouts: 35.8 us -> 11.7 us
  starting transfers between devices: 34.7 us -> 16.6 us
  between operations: 14.7 us -> 0.92 us
  other arithmetic: 11.8 us -> 3.72 us
  Pallas kernels: 0 us -> 7.39 us
    psum x1 -> x0, waiting for transfers between devices: 31.5 us -> none  [from_root(): return lax.psum(jnp.where(mine, value, jnp.zeros_like(value)), axis)]
    slice x42 -> x0, local copies, waits for them, and re-layouts: 14.9 us -> none  [the longest x9 6.94 us: rate(): stress[1]]
    ppermute x6 -> x3, starting transfers between devices: 17.7 us -> 3.71 us  [the longest x2 3.11 us: swap_edges(): got = lax.ppermute(jnp.where(upper, tail, head), 'tile', pairs)]
    broadcast_in_dim x12 -> x0, local copies, waits for them, and re-layouts: 7.91 us -> none  [the longest x6 7.37 us: upsample(): jnp.repeat(jnp.repeat(panel, 2, axis=-2), 2, axis=-1).astype(jnp.float32)]
    pallas_call x0 -> x2, Pallas kernels: none -> 7.39 us  [the longest x1 4.15 us: step(): pl.pallas_call(functools.partial(step_kernel, total_rows), out_shape=jax....]
    reshape x2 -> x0, local copies, waits for them, and re-layouts: 4.39 us -> none  [the longest x1 3.95 us: body(): states.reshape(part_dev, dom_size, -1)]
    all_to_all x2, starting transfers between devices: 16.8 us -> 12.9 us  [the longest x1 7.39 us: exchange_all(): lax.all_to_all(cells, 'dom', split_axis=3, concat_axis=0, tiled=True)]
    all_to_all x1 -> x0, other arithmetic: 3.78 us -> none  [body(): lax.all_to_all(picked, 'dom', split_axis=0, concat_axis=1, tiled=True)]
  transfers between devices with their start and end apart: 9 -> 5, of which waited for: 5 -> 3; matrix products, arithmetic and copies ran while one was open for 15% -> 3% of each run, Pallas kernels for 0% -> 4%
where the time goes in v1:
time: 74.3 us; the launch traced here: 73.9 us
  waiting for transfers between devices  33.6 us (45%)
  starting transfers between devices  16.6 us (22%)
  local copies, waits for them, and re-layouts  11.7 us (16%)
  Pallas kernels  7.39 us (10%)
  other arithmetic  3.72 us (5%)
  between operations  0.92 us (1%)
    all_to_all x1, waiting for transfers between devices, exchange_all(): lax.all_to_all(cells, 'dom', split_axis=3, concat_axis=0, tiled=True)  18.3 us
    all_to_all x1, waiting for transfers between devices, exchange_all(): lax.all_to_all(picked, 'dom', split_axis=0, concat_axis=3, tiled=True)  14.6 us
    all_to_all x1, starting transfers between devices, exchange_all(): lax.all_to_all(cells, 'dom', split_axis=3, concat_axis=0, tiled=True)  7.39 us
    all_to_all x1, starting transfers between devices, exchange_all(): lax.all_to_all(picked, 'dom', split_axis=0, concat_axis=3, tiled=True)  5.47 us
    unnamed x8, local copies, waits for them, and re-layouts  4.24 us
    pallas_call x1, Pallas kernels, step(): pl.pallas_call(functools.partial(step_kernel, total_rows), out_shape=jax....  4.15 us
    pallas_call x1, Pallas kernels, fine_wind(): pl.pallas_call(wind_kernel, out_shape=jax.ShapeDtypeStruct((hours, parts,...  3.24 us
    ppermute x2, starting transfers between devices, swap_edges(): got = lax.ppermute(jnp.where(upper, tail, head), 'tile', pairs)  3.11 us
  transfers between devices with their start and end apart: 5, of which 3 were waited for; matrix products, arithmetic and copies ran while one was open for 3% of the time, Pallas kernels for 4%

profile of v1, /device:TPU:0, one launch (start us, length us, event | category | flops | bytes accessed | tf_op | source)
XLA Modules:
  0.0 73.9 jit_solution(16166009165575956951)
XLA Ops:
  0.0 1.5 %convert_element_type.18 = f16[1,3,64,2048]{3,2,1,0:T(8,128)(2,1)S(1)} convert(f32[1,3,64,2048]{3,2,1,0:T(8,128)} %param.5) | non-fusion elementwise | flops 393216 | bytes 2359296 | tf_op jit(solution)/shard_map/convert_element_type | solution.py:223
  1.5 2.0 %copy.23 = f16[1,3,64,2048]{2,1,0,3:T(4,128)(2,1)S(1)} copy(f16[1,3,64,2048]{3,2,1,0:T(8,128)(2,1)S(1)} %convert_element_type.18) | data formatting | bytes 1572864 | tf_op jit(solution)/shard_map/convert_element_type | solution.py:223
  3.5 2.6 %reshape.118 = f16[16,2,12288]{2,1,0:T(2,128)(2,1)} reshape(f16[2048,1,3,64]{3,2,1,0:T(4,128)(2,1)S(1)} %bitcast.21) | data formatting | bytes 1572864
  6.1 7.4 %all-to-all-start = ((f16[16,2,12288]{2,1,0:T(2,128)(2,1)}), f16[16,2,12288]{2,1,0:T(2,128)(2,1)S(1)}, u32[]{:S(2)}, u32[]{:S(2)}) async-start(f16[16,2,12288]{2,1,0:T(2,128)(2,1)} %reshape.118), calls=%async_computation | async-start | bytes 1572864 | tf_op jit(solution)/shard_map/all_to_all | solution.py:204
  13.7 0.1 reduce
  13.8 0.1 convert_reduce_fusion
  13.9 18.3 %all-to-all-done = f16[16,2,12288]{2,1,0:T(2,128)(2,1)S(1)} async-done(((f16[16,2,12288]{2,1,0:T(2,128)(2,1)}), f16[16,2,12288]{2,1,0:T(2,128)(2,1)S(1)}, u32[]{:S(2)}, u32[]{:S(2)}) %all-to-all-start) | async-done | bytes 786464 | tf_op jit(solution)/shard_map/all_to_all | solution.py:204
  32.2 1.6 %reshape.119 = f16[2048,1,3,64]{3,2,1,0:T(4,128)(2,1)S(1)} reshape(f16[16,2,12288]{2,1,0:T(2,128)(2,1)S(1)} %all-to-all-done) | data formatting | bytes 1572864
  33.8 2.3 %copy.25 = f16[1,3,64,16,128]{4,2,1,3,0:T(8,128)(2,1)} copy(f16[1,3,64,16,128]{2,1,4,3,0:T(4,128)(2,1)S(1)} %bitcast.22) | data formatting | bytes 1572864 | tf_op jit(solution)/shard_map/all_to_all | solution.py:204
  36.1 2.0 %gather_fusion = f16[16,3,64,128]{3,2,1,0:T(8,128)(2,1)S(1)} fusion(f16[16,3,64,128]{3,2,1,0:T(8,128)(2,1)} %bitcast.24, s32[1024]{0:T(1024)S(1)} %pad_clamp_fusion), kind=kCustom, calls=%fused_computation | custom fusion | bytes 1572928 | tf_op jit(solution)/shard_map/jit(_take)/gather | solution.py:205
  38.2 1.2 %broadcast_select_fusion = f16[16,3,64,128]{3,2,1,0:T(8,128)(2,1)} fusion(f16[16,3,64,128]{3,2,1,0:T(8,128)(2,1)S(1)} %gather_fusion, pred[16]{0:T(512)(128)(4,1)S(1)} %compare_and_fusion), kind=kLoop, calls=%fused_computation.8 | loop fusion | flops 393216 | bytes 1572880 | tf_op jit(solution)/shard_map/jit(_take)/select_n | solution.py:205
  39.3 5.5 %all-to-all-start.1 = ((f16[16,3,64,128]{3,2,1,0:T(8,128)(2,1)}), f16[16,3,64,128]{3,2,1,0:T(8,128)(2,1)S(1)}, u32[]{:S(2)}, u32[]{:S(2)}) async-start(f16[16,3,64,128]{3,2,1,0:T(8,128)(2,1)} %broadcast_select_fusion), calls=%async_computation.1 | async-start | bytes 1572864 | tf_op jit(solution)/shard_map/all_to_all | solution.py:206
  44.8 1.6 %collective-permute-start.1 = (f32[3,2048]{1,0:T(4,128)S(1)}, f32[3,2048]{1,0:T(4,128)S(1)}, u32[]{:S(2)}, u32[]{:S(2)}) collective-permute-start(f32[3,2048]{1,0:T(4,128)S(1)} %slice_select_fusion.1), channel_id=1, source_target_pairs={{0,1},{1,0},{2,3},{3,2},{4,5},{5,4},{6,7},{7,6},{8,9},{9,8},{10,11... | collective-permute-start | bytes 73736 | tf_op jit(solution)/shard_map/ppermute | solution.py:35
  47.1 0.2 constant_dynamic-slice_fusion.1
  47.4 0.6 collective-permute-start.2
  48.2 0.7 collective-permute-done.1
  48.9 14.6 %all-to-all-done.1 = f16[16,3,64,128]{3,2,1,0:T(8,128)(2,1)S(1)} async-done(((f16[16,3,64,128]{3,2,1,0:T(8,128)(2,1)}), f16[16,3,64,128]{3,2,1,0:T(8,128)(2,1)S(1)}, u32[]{:S(2)}, u32[]{:S(2)}) %all-to-all-start.1) | async-done | bytes 786464 | tf_op jit(solution)/shard_map/all_to_all | solution.py:206
  63.5 0.5 copy.26
  64.0 0.4 squeeze.2
  64.5 1.6 %collective-permute-start = (f16[3,3,2048]{2,1,0:T(4,128)(2,1)S(1)}, f16[3,3,2048]{2,1,0:T(4,128)(2,1)S(1)}, u32[]{:S(2)}, u32[]{:S(2)}) collective-permute-start(f16[3,3,2048]{2,1,0:T(4,128)(2,1)S(1)} %slice_select_fusion), channel_id=1, source_target_pairs={{0,1},{1,0},{2,3},{3,2},{4,5},{5,4},{6,7},{7,6},{8,9},{9,8},{10,11... | collective-permute-start | bytes 110600 | tf_op jit(solution)/shard_map/ppermute | solution.py:35
  66.1 0.1 maximum_select_fusion.coarse_ref
  66.2 3.2 %shard_map.55.wind_ref = f32[2,2,80,2048]{3,2,1,0:T(8,128)S(1)} custom-call(s32[2]{0:T(128)S(1)} %pad_add_fusion.where_ref, bf16[2,2,48,1024]{3,2,1,0:T(8,128)(2,1)S(1)} %maximum_select_fusion.coarse_ref), custom_call_target="tpu_custom_call" | custom-call | flops 62914560 | bytes 2621440 | tf_op jit(solution)/shard_map/pallas_call | solution.py:98
  69.5 0.2 fusion.3.state_ref
  69.7 4.1 %shard_map.56 = f32[3,64,2048]{2,1,0:T(8,128)} custom-call(s32[1]{0:T(128)} %bitcast.where_ref, f32[3,80,2048]{2,1,0:T(8,128)S(1)} %fusion.3.state_ref, f32[80,2048]{1,0:T(8,128)S(1)} %fusion.5.depth_ref, f32[2,2,80,2048]{3,2,1,0:T(8,128)S(1)} %shard_map.55.wind_ref), custom_call_target="tpu_custom_call" | custom-call | flops 49152000 | bytes 7864320 | tf_op jit(solution)/shard_map/pallas_call | solution.py:184
  (21 shorter events, 0.6 us)
Async XLA Ops:
  3.5 10.0 %copy-start.2 = (s32[16]{0:T(128)S(1)}, s32[16]{0:T(128)}, u32[]{:S(2)}) copy-start(s32[16]{0:T(128)} %param.6) | copy-start | bytes 196
  6.1 26.1 %all-to-all-start = ((f16[16,2,12288]{2,1,0:T(2,128)(2,1)}), f16[16,2,12288]{2,1,0:T(2,128)(2,1)S(1)}, u32[]{:S(2)}, u32[]{:S(2)}) async-start(f16[16,2,12288]{2,1,0:T(2,128)(2,1)} %reshape.118), calls=%async_computation | async-start | bytes 1572864 | tf_op jit(solution)/shard_map/all_to_all | solution.py:204
  38.1 6.7 %copy-start.1 = (f32[64,2048]{1,0:T(8,128)S(1)}, f32[64,2048]{1,0:T(8,128)}, u32[]{:S(2)}) copy-start(f32[64,2048]{1,0:T(8,128)} %param.7) | copy-start | bytes 1572868
  38.1 9.0 %copy-start = (bf16[3,2,64,1024]{3,2,1,0:T(8,128)(2,1)S(1)}, bf16[3,2,64,1024]{3,2,1,0:T(8,128)(2,1)}, u32[]{:S(2)}) copy-start(bf16[3,2,64,1024]{3,2,1,0:T(8,128)(2,1)} %param.8) | copy-start | bytes 2359300
  39.3 24.2 %all-to-all-start.1 = ((f16[16,3,64,128]{3,2,1,0:T(8,128)(2,1)}), f16[16,3,64,128]{3,2,1,0:T(8,128)(2,1)S(1)}, u32[]{:S(2)}, u32[]{:S(2)}) async-start(f16[16,3,64,128]{3,2,1,0:T(8,128)(2,1)} %broadcast_select_fusion), calls=%async_computation.1 | async-start | bytes 1572864 | tf_op jit(solution)/shard_map/all_to_all | solution.py:206
  44.8 4.0 %collective-permute-start.1 = (f32[3,2048]{1,0:T(4,128)S(1)}, f32[3,2048]{1,0:T(4,128)S(1)}, u32[]{:S(2)}, u32[]{:S(2)}) collective-permute-start(f32[3,2048]{1,0:T(4,128)S(1)} %slice_select_fusion.1), channel_id=1, source_target_pairs={{0,1},{1,0},{2,3},{3,2},{4,5},{5,4},{6,7},{7,6},{8,9},{9,8},{10,11... | collective-permute-start | bytes 73736 | tf_op jit(solution)/shard_map/ppermute | solution.py:35
  47.4 18.7 %collective-permute-start.2 = (bf16[2,2,48,1024]{3,2,1,0:T(8,128)(2,1)S(1)}, bf16[2,2,48,1024]{3,2,1,0:T(8,128)(2,1)S(1)}, u32[]{:S(2)}, u32[]{:S(2)}) collective-permute-start(bf16[2,2,48,1024]{3,2,1,0:T(8,128)(2,1)S(1)} %pad_maximum_fusion), channel_id=1, source_target_pairs={{0,1},{1,0},{2,3},{3,2},{4,5},{5,4},{6,7},{7,6},{8,9},{9,8},{10,11... | collective-permute-start | bytes 1179656 | tf_op jit(solution)/shard_map/ppermute | solution.py:66
  64.5 4.9 %collective-permute-start = (f16[3,3,2048]{2,1,0:T(4,128)(2,1)S(1)}, f16[3,3,2048]{2,1,0:T(4,128)(2,1)S(1)}, u32[]{:S(2)}, u32[]{:S(2)}) collective-permute-start(f16[3,3,2048]{2,1,0:T(4,128)(2,1)S(1)} %slice_select_fusion), channel_id=1, source_target_pairs={{0,1},{1,0},{2,3},{3,2},{4,5},{5,4},{6,7},{7,6},{8,9},{9,8},{10,11... | collective-permute-start | bytes 110600 | tf_op jit(solution)/shard_map/ppermute | solution.py:35

commit v2 on v1

--- a/solution.py
+++ b/solution.py
@@ -12,6 +12,7 @@
 EDGE = 3
 PAD = 8
 VMEM_BYTES = 48 * 1024 * 1024
+CHUNKS = 1
 
 
 def parent_list(offspring):
@@ -40,39 +41,46 @@
 
 def wind_window(wind, start_hour, row_count):
     count = lax.axis_size("tile")
+    devices = lax.axis_size("dom")
     me = lax.axis_index("tile")
     hours_dev, parts, coarse_rows, coarse_cols = wind.shape
     own_rows = row_count // 2
-    window = min(own_rows + 2 * PAD, coarse_rows)
+    window = min(own_rows + PAD, coarse_rows)
+    shared = devices % 2 == 0
+    odd = lax.axis_index("dom") % 2
 
     def first_row(tile):
-        return jnp.clip(tile * own_rows - PAD, 0, coarse_rows - window)
-
-    hours = [start_hour[0], start_hour[0] + 1]
-
-    def panels(tile):
-        return jnp.concatenate(
-            [
-                lax.dynamic_slice(
-                    wind, (hour % hours_dev, 0, first_row(tile), 0), (1, parts, window, coarse_cols)
-                )
-                for hour in hours
-            ]
+        return jnp.clip(tile * own_rows - PAD // 2, 0, coarse_rows - window)
+
+    def panel(hour, tile):
+        cells = lax.dynamic_slice(
+            wind, (hour % hours_dev, 0, first_row(tile), 0), (1, parts, window, coarse_cols)
         )
-
-    owner = jnp.stack(hours)[:, None, None, None] // hours_dev
-    found = panels(me)
-    for shift in range(1, count):
-        got = lax.ppermute(
-            panels((me + shift) % count), "tile", [(i, (i + shift) % count) for i in range(count)]
-        )
-        found = jnp.where(owner == (me - shift) % count, got, found)
-    return found, first_row(me)
+        return cells.reshape(parts * window, coarse_cols)
+
+    def fetch(hour):
+        found = panel(hour, me)
+        for shift in range(1, count):
+            got = lax.ppermute(
+                panel(hour, (me + shift) % count),
+                "tile",
+                [(i, (i + shift) % count) for i in range(count)],
+            )
+            found = jnp.where(hour // hours_dev == (me - shift) % count, got, found)
+        return found
+
+    if not shared:
+        return jnp.concatenate([fetch(start_hour[0]), fetch(start_hour[0] + 1)]), first_row(me)
+    found = fetch(start_hour[0] + odd)
+    other = lax.ppermute(found, "dom", [(i, i ^ 1) for i in range(devices)])
+    both = [jnp.where(odd == 0, found, other), jnp.where(odd == 0, other, found)]
+    return jnp.concatenate(both), first_row(me)
 
 
 def wind_kernel(where_ref, coarse_ref, fine_ref):
-    hours, parts, window, coarse_cols = coarse_ref.shape
-    rows = fine_ref.shape[2]
+    hours, parts, rows, fine_cols = fine_ref.shape
+    coarse_cols = fine_cols // 2
+    window = coarse_ref.shape[0] // (hours * parts)
     first = where_ref[0]
     base = where_ref[1]
     fine_row = lax.broadcasted_iota(jnp.int32, (rows, window), 0) + first
@@ -82,19 +90,20 @@
     fine_col = lax.broadcasted_iota(jnp.int32, (step, 2 * step), 1)
     coarse_col = lax.broadcasted_iota(jnp.int32, (step, 2 * step), 0)
     widen = jnp.where((fine_col >> 1) == coarse_col, 1.0, 0.0).astype(jnp.bfloat16)
-    for hour in range(hours):
-        for part in range(parts):
-            for left in range(0, coarse_cols, step):
-                cells = coarse_ref[hour, part, :, left : left + step]
-                wide = jnp.dot(cells, widen, preferred_element_type=jnp.float32)
-                tall = jnp.dot(
-                    lift, wide.astype(jnp.bfloat16), preferred_element_type=jnp.float32
-                )
+    for left in range(0, coarse_cols, step):
+        cells = coarse_ref[:, left : left + step]
+        wide_cells = jnp.dot(cells, widen, preferred_element_type=jnp.float32)
+        for hour in range(hours):
+            for part in range(parts):
+                low = (hour * parts + part) * window
+                panel = wide_cells[low : low + window].astype(jnp.bfloat16)
+                tall = jnp.dot(lift, panel, preferred_element_type=jnp.float32)
                 fine_ref[hour, part, :, 2 * left : 2 * (left + step)] = TIME_STEP * tall
 
 
 def fine_wind(coarse, first, base, rows):
-    hours, parts, window, cols = coarse.shape
+    hours, parts = 2, 2
+    window, cols = coarse.shape[0] // (hours * parts), coarse.shape[1]
     return pl.pallas_call(
         wind_kernel,
         out_shape=jax.ShapeDtypeStruct((hours, parts, rows, 2 * cols), jnp.float32),
@@ -201,36 +210,163 @@
 
 
 def exchange_all(cells, parents):
-    spread = lax.all_to_all(cells, "dom", split_axis=3, concat_axis=0, tiled=True)
+    spread = lax.all_to_all(cells[None], "dom", split_axis=3, concat_axis=0, tiled=True)
     picked = jnp.take(spread, parents, axis=0)
-    return lax.all_to_all(picked, "dom", split_axis=0, concat_axis=3, tiled=True)
+    return lax.all_to_all(picked, "dom", split_axis=0, concat_axis=3, tiled=True)[0]
+
+
+def wide(array):
+    return array.astype(jnp.float32)
+
+
+def unit_of(pool, unit):
+    return jnp.where(unit == 0, wide(pool[0])[None], wide(pool[1])[None])
+
+
+class Near:
+    def __init__(self):
+        self.count = lax.axis_size("dom")
+        self.groups = self.count // 4
+        me = lax.axis_index("dom")
+        self.group, self.pair, self.core = me // 4, me // 2 % 2, me % 2
+        self.first = self.core == 0
+        self.even_group = self.group ^ 1
+        self.odd_group = ((self.group + 1) ^ 1) - 1
+
+    def move(self, array, pairs):
+        return lax.ppermute(array, "dom", pairs) if pairs else array
+
+    def neighbour(self):
+        return [(i, i ^ 1) for i in range(self.count)]
+
+    def across(self, which):
+        return [(i, i ^ 2) for i in range(self.count) if i % 2 == which]
+
+    def along(self, which, parity):
+        lower = [
+            i
+            for i in range(self.count - 4)
+            if i % 2 == which and i // 4 % 2 == parity
+        ]
+        return [(i, i + 4) for i in lower] + [(i + 4, i) for i in lower]
+
+    def halves(self, state):
+        half = state.shape[1] // 2
+        keep = lax.dynamic_slice_in_dim(state, self.core * half, half, 1)
+        send = lax.dynamic_slice_in_dim(state, (1 - self.core) * half, half, 1)
+        return keep, send.astype(jnp.float16)
+
+    def pair_halves(self, keep, got):
+        own = jnp.arange(2).reshape(2, 1, 1, 1) == self.core
+        return jnp.where(own, keep[None], wide(got)[None]).astype(jnp.float16)
+
+    def first_round(self, mine):
+        one = self.move(mine, self.across(0) + self.along(1, 0))
+        two = self.move(mine, self.along(1, 1))
+        return mine, one, two
+
+    def held(self, pools, parent):
+        mine, one, two = lax.optimization_barrier(pools)
+        unit = parent % 2
+        place = parent // 4
+        in_one = jnp.where(self.first, parent // 2 % 2 != self.pair, place == self.even_group)
+        in_two = ~self.first & (place == self.odd_group) & ~in_one
+        rest = jnp.where(in_one, unit_of(one, unit), unit_of(mine, unit))
+        return jnp.where(in_two, unit_of(two, unit), rest)
+
+    def wanted(self, parents, to_group, to_pair):
+        base = 4 * jnp.clip(to_group, 0, self.groups - 1) + 2 * to_pair
+        return lax.dynamic_slice_in_dim(parents, base, 2).reshape(2, 1, 1, 1)
+
+    def second_round(self, pools, parents):
+        first, pair = self.first, self.pair
+        to_even = self.wanted(
+            parents,
+            jnp.where(first, self.even_group, self.group),
+            jnp.where(first, pair, 1 - pair),
+        )
+        to_odd = self.wanted(parents, self.odd_group, pair)
+        send = self.held(pools, to_even).astype(jnp.float16)
+        three = self.move(send, self.along(0, 0) + self.across(1))
+        send = self.held(pools, to_odd).astype(jnp.float16)
+        four = self.move(send, self.along(0, 1))
+        return three, four
+
+    def slots(self, pools, three, four, parents):
+        first = self.first
+        parent = self.wanted(parents, self.group, self.pair)
+        place = parent // 4
+        in_three = jnp.where(first, place == self.even_group, parent // 2 % 2 != self.pair)
+        in_four = first & (place == self.odd_group) & (place != self.group) & ~in_three
+        both = jnp.where(in_three, wide(three), self.held(pools, parent))
+        both = jnp.where(in_four, wide(four), both)
+        own = jnp.where(first, both[0], both[1]).astype(jnp.float16)
+        return own, jnp.where(first, both[1], both[0]).astype(jnp.float16)
 
 
 def body(states, offspring, sea_depth, wind, start_hour):
     row_count = states.shape[2]
     total_rows = row_count * lax.axis_size("tile")
     first = lax.axis_index("tile") * row_count - PAD
+    rows = row_count + 2 * PAD
+    fill = ((PAD - EDGE, 0), (0, 0)), ((0, PAD - EDGE), (0, 0))
     parents = parent_list(offspring)
-    coarse, base = wind_window(wind, start_hour, row_count)
-    rows = row_count + 2 * PAD
-    stress = fine_wind(coarse, first, base, rows)
-    fill = ((PAD - EDGE, 0), (0, 0)), ((0, PAD - EDGE), (0, 0))
-
-    depth_above, depth_below = swap_edges(sea_depth[:EDGE], sea_depth[-EDGE:])
-    depth = (0.5 * TIME_STEP) * jnp.concatenate(
-        [jnp.pad(depth_above, fill[0]), sea_depth, jnp.pad(depth_below, fill[1])]
-    )
-    copied = exchange_all(states.astype(jnp.float16), parents)[0]
-    above, below = swap_edges(copied[:, :EDGE], copied[:, -EDGE:])
-    state = jnp.concatenate(
-        [
-            jnp.pad(above, ((0, 0),) + fill[0]),
-            copied,
-            jnp.pad(below, ((0, 0),) + fill[1]),
-        ],
-        axis=1,
-    ).astype(jnp.float32)
-    return step(state, depth, stress, first, total_rows)[None]
+    slots = jnp.arange(parents.shape[0], dtype=jnp.int32)
+    state = states[0]
+
+    def surroundings(sea_depth, wind):
+        coarse, base = wind_window(wind, start_hour, row_count)
+        above, below = swap_edges(sea_depth[:EDGE], sea_depth[-EDGE:])
+        return coarse, base, above, below
+
+    def fields(sea_depth, coarse, base, above, below):
+        depth = (0.5 * TIME_STEP) * jnp.concatenate(
+            [jnp.pad(above, fill[0]), sea_depth, jnp.pad(below, fill[1])]
+        )
+        return depth, fine_wind(coarse, first, base, rows)
+
+    def finish(parts, depth, stress):
+        above, below = swap_edges(parts[0][:, :EDGE], parts[-1][:, -EDGE:])
+        pieces = [jnp.pad(wide(above), ((0, 0),) + fill[0])]
+        pieces += [wide(part) for part in parts]
+        pieces += [jnp.pad(wide(below), ((0, 0),) + fill[1])]
+        return step(jnp.concatenate(pieces, axis=1), depth, stress, first, total_rows)
+
+    def far():
+        around = surroundings(sea_depth, wind)
+        copied = exchange_all(state.astype(jnp.float16), parents)
+        return finish([copied], *fields(sea_depth, *around))
+
+    def near():
+        plan = Near()
+        keep, send = plan.halves(state)
+        got = plan.move(send, plan.neighbour())
+        size = keep.shape[1] // CHUNKS
+        pools = [
+            plan.first_round(plan.pair_halves(keep[:, at : at + size], got[:, at : at + size]))
+            for at in range(0, CHUNKS * size, size)
+        ]
+        mine, later_depth, later_wind = lax.optimization_barrier(
+            ([pool[0] for pool in pools], sea_depth, wind)
+        )
+        pools = [(own,) + pool[1:] for own, pool in zip(mine, pools)]
+        around = surroundings(later_depth, later_wind)
+        pools[-1], around = lax.optimization_barrier((pools[-1], around))
+        moved = [plan.second_round(pool, parents) for pool in pools]
+        depth, stress = fields(sea_depth, *around)
+        moved[-1], depth, stress = lax.optimization_barrier((moved[-1], depth, stress))
+        upper, lower = [], []
+        for pool, (three, four) in zip(pools, moved):
+            own, other = plan.slots(pool, three, four, parents)
+            other = plan.move(other, plan.neighbour())
+            upper.append(jnp.where(plan.first, wide(own), wide(other)).astype(jnp.float16))
+            lower.append(jnp.where(plan.first, wide(other), wide(own)).astype(jnp.float16))
+        return finish(upper + lower, depth, stress)
+
+    if parents.shape[0] % 4 or row_count % (2 * CHUNKS):
+        return far()[None]
+    close = jnp.all(jnp.abs(parents // 4 - slots // 4) <= 1)
+    return lax.cond(close, near, far)[None]
 
 
 def solution(mesh):

time: 74.3 us -> 48.6 us (0.65)
  waiting for transfers between devices: 33.6 us -> 16.9 us
  local copies, waits for them, and re-layouts: 11.7 us -> 2.97 us
  Pallas kernels: 7.39 us -> 5.13 us
  other arithmetic: 3.72 us -> 5.68 us
  loops' own time: 0 us -> 1.19 us
  starting transfers between devices: 16.6 us -> 15.8 us
    all_to_all x2 -> x0, waiting for transfers between devices: 32.9 us -> none  [the longest x1 18.3 us: exchange_all(): lax.all_to_all(cells, 'dom', split_axis=3, concat_axis=0, tiled=True)]
    ppermute x1 -> x8, waiting for transfers between devices: 0.01 us -> 14.3 us  [the longest x6 9.86 us: move(): return lax.ppermute(array, 'dom', pairs) if pairs else array]
    ppermute x1 -> x8, starting transfers between devices: 0.6 us -> 13.6 us  [the longest x6 10.1 us: move(): return lax.ppermute(array, 'dom', pairs) if pairs else array]
    all_to_all x2 -> x0, starting transfers between devices: 12.9 us -> none  [the longest x1 7.39 us: exchange_all(): lax.all_to_all(cells, 'dom', split_axis=3, concat_axis=0, tiled=True)]
    unnamed x8 -> x2, local copies, waits for them, and re-layouts: 4.24 us -> 1.14 us
    all_to_all x2 -> x0, local copies, waits for them, and re-layouts: 2.8 us -> none  [the longest x1 2.28 us: exchange_all(): lax.all_to_all(cells, 'dom', split_axis=3, concat_axis=0, tiled=True)]
    gather x1 -> x0, local copies, waits for them, and re-layouts: 2.02 us -> none  [exchange_all(): picked = jnp.take(spread, parents, axis=0)]
    convert_element_type x1 -> x0, local copies, waits for them, and re-layouts: 1.95 us -> none  [body(): copied = exchange_all(states.astype(jnp.float16), parents)[0]]
  transfers between devices with their start and end apart: 5 -> 10, of which waited for: 3 -> 7; matrix products, arithmetic and copies ran while one was open for 3% -> 3% of each run, Pallas kernels for 4% -> 4%
where the time goes in v2:
time: 48.6 us; the launch traced here: 48.4 us
  waiting for transfers between devices  16.9 us (35%)
  starting transfers between devices  15.8 us (33%)
  other arithmetic  5.68 us (12%)
  Pallas kernels  5.13 us (11%)
  local copies, waits for them, and re-layouts  2.97 us (6%)
  loops' own time  1.19 us (2%)
  between operations  0.67 us (1%)
    ppermute x6, starting transfers between devices, move(): return lax.ppermute(array, 'dom', pairs) if pairs else array  10.1 us
    ppermute x6, waiting for transfers between devices, move(): return lax.ppermute(array, 'dom', pairs) if pairs else array  9.86 us
    ppermute x1, waiting for transfers between devices, fetch(): lax.ppermute(panel(hour, (me + shift) % count), 'tile', [(i, (i + shift)...  3.47 us
    pallas_call x1, Pallas kernels, step(): pl.pallas_call(functools.partial(step_kernel, total_rows), out_shape=jax....  3 us
    ppermute x2, waiting for transfers between devices, swap_edges(): got = lax.ppermute(jnp.where(upper, tail, head), 'tile', pairs)  2.6 us
    ppermute x2, starting transfers between devices, swap_edges(): got = lax.ppermute(jnp.where(upper, tail, head), 'tile', pairs)  2.16 us
    pallas_call x1, Pallas kernels, fine_wind(): pl.pallas_call(wind_kernel, out_shape=jax.ShapeDtypeStruct((hours, parts,...  2.12 us
    ppermute x1, starting transfers between devices, wind_window(): other = lax.ppermute(found, 'dom', [(i, i ^ 1) for i in range(devices)])  2.03 us
  transfers between devices with their start and end apart: 10, of which 7 were waited for; matrix products, arithmetic and copies ran while one was open for 3% of the time, Pallas kernels for 4%

profile of v2, /device:TPU:0, one launch (start us, length us, event | category | flops | bytes accessed | tf_op | source)
XLA Modules:
  0.0 48.4 jit_solution(4390130084348326172)
XLA Ops:
  0.0 0.7 %copy.22 = s32[16,1]{1,0:T(8,128)S(1)} copy(s32[16,1]{0,1:T(1,128)} %bitcast.63) | data formatting | bytes 128 | tf_op jit(solution)/shard_map/reshape.219
  1.0 0.7 %compare_reduce_fusion = pred[]{:T(512)} fusion(s32[16]{0:T(128)S(1)} %convert_reduce_fusion), kind=kLoop, calls=%fused_computation.129 | loop fusion | flops 431 | bytes 65 | tf_op jit(solution)/shard_map/reduce_and | solution.py:368
  2.3 44.9 %conditional.1 = (f32[1,3,64,2048]{3,2,1,0:T(8,128)S(1)}) conditional(s32[]{:T(128)} %convert_element_type.101, (s32[]{:T(128)}, s32[16]{0:T(128)S(1)}, f32[3,64,2048]{2,1,0:T(8,128)}, f32[64,2048]{1,0:T(8,128)}, s32[1]{0:T(128)}, /*index=5*/bf16[3,2,64,1024]{3,2,1,0:T(8,128)(2,1)}) %tuple.56, (s32[]{:T(128)}, s32[16]{0:T(128)S(1)}, ...), branch_computations={%region_3.4_spmd, %region_4.5_spmd} | conditional | flops 120611248 | bytes 70175896 | solution.py:369
  2.4 1.5 %constant_dynamic-slice_fusion.2 = (f32[3,32,2048]{2,1,0:T(8,128)S(1)}, f16[3,32,2048]{2,1,0:T(8,128)(2,1)S(1)}) fusion(f32[3,64,2048]{2,1,0:T(8,128)} %get-tuple-element.41, s32[]{:T(128)S(6)} %select_n.326, s32[]{:T(128)S(6)} %select_n.327), kind=kLoop, calls=%fused_computation.71 | loop fusion | flops 196608 | bytes 2752520 | tf_op jit(solution)/shard_map/cond/branch_1_fun/dynamic_slice | solution.py:255
  3.8 0.5 %collective-permute-start = (f16[3,32,2048]{2,1,0:T(8,128)(2,1)S(1)}, f16[3,32,2048]{2,1,0:T(8,128)(2,1)S(1)}, u32[]{:S(2)}, u32[]{:S(2)}) collective-permute-start(f16[3,32,2048]{2,1,0:T(8,128)(2,1)S(1)} %get-tuple-element.99), channel_id=1, source_target_pairs={{0,2},{2,0},{4,6},{6,4},{8,10},{10,8},{12,14},{14,12},{16,18},{18,... | collective-permute-start | bytes 1179656 | tf_op jit(solution)/shard_map/cond/branch_1_fun/ppermute | solution.py:237
  6.0 0.7 %collective-permute-start.2 = (f16[2,3,32,2048]{3,2,1,0:T(8,128)(2,1)S(1)}, f16[2,3,32,2048]{3,2,1,0:T(8,128)(2,1)S(1)}, u32[]{:S(2)}, u32[]{:S(2)}) collective-permute-start(f16[2,3,32,2048]{3,2,1,0:T(8,128)(2,1)S(1)} %select_convert_fusion.2), channel_id=1, source_target_pairs={{10,18},{14,22},{18,10},{22,14},{11,19},{15,23},{19,11},{23,15}} | collective-permute-start | bytes 2359304 | tf_op jit(solution)/shard_map/cond/branch_1_fun/ppermute | solution.py:237
  6.7 3.0 %collective-permute-start.1 = (f16[2,3,32,2048]{3,2,1,0:T(8,128)(2,1)S(1)}, f16[2,3,32,2048]{3,2,1,0:T(8,128)(2,1)S(1)}, u32[]{:S(2)}, u32[]{:S(2)}) collective-permute-start(f16[2,3,32,2048]{3,2,1,0:T(8,128)(2,1)S(1)} %select_convert_fusion.2), channel_id=1, source_target_pairs={{0,4},{4,0},{8,12},{12,8},{16,20},{20,16},{24,28},{28,24},{2,10},{... | collective-permute-start | bytes 2359304 | tf_op jit(solution)/shard_map/cond/branch_1_fun/ppermute | solution.py:237
  9.7 1.1 %constant_dynamic-slice_fusion = (bf16[1,2,40,1024]{3,2,1,0:T(8,128)(2,1)S(1)}, bf16[1,2,40,1024]{3,2,1,0:T(8,128)(2,1)S(1)}) fusion(bf16[3,2,64,1024]{3,2,1,0:T(8,128)(2,1)} %get-tuple-element.46, s32[]{:T(128)S(6)} %select_n.334, s32[]{:T(128)} %min.22, s32[]{:T(128)S(6)} %min.21), kind=kLoop, calls=%fused_computation.69 | loop fusion | bytes 655372 | tf_op jit(solution)/shard_map/cond/branch_1_fun/dynamic_slice | solution.py:56
  10.8 1.6 %collective-permute-start.3 = (bf16[80,1024]{1,0:T(8,128)(2,1)S(1)}, bf16[80,1024]{1,0:T(8,128)(2,1)S(1)}, u32[]{:S(2)}, u32[]{:S(2)}) collective-permute-start(bf16[80,1024]{1,0:T(8,128)(2,1)S(1)} %bitcast.62), channel_id=1, source_target_pairs={{0,1},{1,0},{2,3},{3,2},{4,5},{5,4},{6,7},{7,6},{8,9},{9,8},{10,11... | collective-permute-start | bytes 491528 | tf_op jit(solution)/shard_map/cond/branch_1_fun/ppermute | solution.py:64
  12.4 0.6 %collective-permute-start.5 = (f32[3,2048]{1,0:T(4,128)S(1)}, f32[3,2048]{1,0:T(4,128)S(1)}, u32[]{:S(2)}, u32[]{:S(2)}) collective-permute-start(f32[3,2048]{1,0:T(4,128)S(1)} %slice_select_fusion.1), channel_id=1, source_target_pairs={{0,1},{1,0},{2,3},{3,2},{4,5},{5,4},{6,7},{7,6},{8,9},{9,8},{10,11... | collective-permute-start | bytes 73736 | tf_op jit(solution)/shard_map/cond/branch_1_fun/ppermute | solution.py:36
  13.0 3.5 %collective-permute-done.3 = bf16[80,1024]{1,0:T(8,128)(2,1)S(1)} collective-permute-done((bf16[80,1024]{1,0:T(8,128)(2,1)S(1)}, bf16[80,1024]{1,0:T(8,128)(2,1)S(1)}, u32[]{:S(2)}, u32[]{:S(2)}) %collective-permute-start.3) | collective-permute-done | bytes 163872 | tf_op jit(solution)/shard_map/cond/branch_1_fun/ppermute | solution.py:64
  16.5 2.0 %collective-permute-start.4 = (bf16[80,1024]{1,0:T(8,128)(2,1)S(1)}, bf16[80,1024]{1,0:T(8,128)(2,1)S(1)}, u32[]{:S(2)}, u32[]{:S(2)}) collective-permute-start(bf16[80,1024]{1,0:T(8,128)(2,1)S(1)} %bitcast_select_fusion), channel_id=1, source_target_pairs={{0,2},{2,0},{4,6},{6,4},{8,10},{10,8},{12,14},{14,12},{16,18},{18,... | collective-permute-start | bytes 491528 | tf_op jit(solution)/shard_map/cond/branch_1_fun/ppermute | solution.py:75
  18.5 1.0 %collective-permute-done.4 = bf16[80,1024]{1,0:T(8,128)(2,1)S(1)} collective-permute-done((bf16[80,1024]{1,0:T(8,128)(2,1)S(1)}, bf16[80,1024]{1,0:T(8,128)(2,1)S(1)}, u32[]{:S(2)}, u32[]{:S(2)}) %collective-permute-start.4) | collective-permute-done | bytes 163872 | tf_op jit(solution)/shard_map/cond/branch_1_fun/ppermute | solution.py:75
  20.1 0.7 %select_convert_fusion = (f16[2,3,32,2048]{3,2,1,0:T(8,128)(2,1)S(1)}, f16[2,3,32,2048]{3,2,1,0:T(8,128)(2,1)S(1)}) fusion(f32[3,32,2048]{2,1,0:T(8,128)S(1)} %get-tuple-element.105, f32[3,32,2048]{2,1,0:T(8,128)S(1)} %get-tuple-element.104, f32[3,32,2048]{2,1,0:T(8,128)S(1)} %get-tuple-element.122, f32[3,32,2048]{2,1,0:T(8,128)S(1)} %get-tuple-element.123, ...), kind=kLoop, calls=%fused_computation.6 | loop fusion | flops 4718592 | bytes 6291468 | tf_op jit(solution)/shard_map/cond/branch_1_fun/convert_element_type | solution.py:291
  20.8 0.9 %collective-permute-start.7 = (f16[2,3,32,2048]{3,2,1,0:T(8,128)(2,1)S(1)}, f16[2,3,32,2048]{3,2,1,0:T(8,128)(2,1)S(1)}, u32[]{:S(2)}, u32[]{:S(2)}) collective-permute-start(f16[2,3,32,2048]{3,2,1,0:T(8,128)(2,1)S(1)} %get-tuple-element.96), channel_id=1, source_target_pairs={{8,16},{12,20},{16,8},{20,12},{9,17},{13,21},{17,9},{21,13}} | collective-permute-start | bytes 2359304 | tf_op jit(solution)/shard_map/cond/branch_1_fun/ppermute | solution.py:237
  21.7 4.9 %collective-permute-start.6 = (f16[2,3,32,2048]{3,2,1,0:T(8,128)(2,1)S(1)}, f16[2,3,32,2048]{3,2,1,0:T(8,128)(2,1)S(1)}, u32[]{:S(2)}, u32[]{:S(2)}) collective-permute-start(f16[2,3,32,2048]{3,2,1,0:T(8,128)(2,1)S(1)} %get-tuple-element.97), channel_id=1, source_target_pairs={{0,8},{4,12},{16,24},{20,28},{8,0},{12,4},{24,16},{28,20},{2,6},{6... | collective-permute-start | bytes 2359304 | tf_op jit(solution)/shard_map/cond/branch_1_fun/ppermute | solution.py:237
  26.7 2.1 %branch_1_fun.2.wind_ref = f32[2,2,80,2048]{3,2,1,0:T(8,128)S(1)} custom-call(s32[2]{0:T(128)S(1)} %pad_add_fusion.where_ref, bf16[160,1024]{1,0:T(8,128)(2,1)S(1)} %pad_maximum_fusion.coarse_ref), custom_call_target="tpu_custom_call" | custom-call | flops 52428800 | bytes 2621440 | tf_op jit(solution)/shard_map/cond/branch_1_fun/pallas_call | solution.py:107
  28.9 7.7 %collective-permute-done.6 = f16[2,3,32,2048]{3,2,1,0:T(8,128)(2,1)S(1)} collective-permute-done((f16[2,3,32,2048]{3,2,1,0:T(8,128)(2,1)S(1)}, f16[2,3,32,2048]{3,2,1,0:T(8,128)(2,1)S(1)}, u32[]{:S(2)}, u32[]{:S(2)}) %collective-permute-start.6) | collective-permute-done | bytes 786464 | tf_op jit(solution)/shard_map/cond/branch_1_fun/ppermute | solution.py:237
  36.6 0.7 %select_select_fusion = f32[2,3,32,2048]{3,2,1,0:T(8,128)S(1)} fusion(f16[2,3,32,2048]{3,2,1,0:T(8,128)(2,1)S(1)} %collective-permute-done.6, f16[2,3,32,2048]{3,2,1,0:T(8,128)(2,1)S(1)} %collective-permute-done.7, f32[3,32,2048]{2,1,0:T(8,128)S(1)} %get-tuple-element.105, f32[3,32,2048]{2,1,0:T(8,128)S(1)} %get-tuple-element.104, ...), kind=kLoop, calls=%fused_computation.5 | loop fusion | flops 3538944 | bytes 7864330 | tf_op jit(solution)/shard_map/cond/branch_1_fun/jit(_where)/select_n | solution.py:302
  37.4 1.7 %collective-permute-done.8 = f16[3,32,2048]{2,1,0:T(8,128)(2,1)S(1)} collective-permute-done((f16[3,32,2048]{2,1,0:T(8,128)(2,1)S(1)}, f16[3,32,2048]{2,1,0:T(8,128)(2,1)S(1)}, u32[]{:S(2)}, u32[]{:S(2)}) %collective-permute-start.8) | collective-permute-done | bytes 393248 | tf_op jit(solution)/shard_map/cond/branch_1_fun/ppermute | solution.py:237
  39.5 1.6 %collective-permute-start.9 = (f16[3,3,2048]{2,1,0:T(4,128)(2,1)S(1)}, f16[3,3,2048]{2,1,0:T(4,128)(2,1)S(1)}, u32[]{:S(2)}, u32[]{:S(2)}) collective-permute-start(f16[3,3,2048]{2,1,0:T(4,128)(2,1)S(1)} %slice_select_fusion), channel_id=1, source_target_pairs={{0,1},{1,0},{2,3},{3,2},{4,5},{5,4},{6,7},{7,6},{8,9},{9,8},{10,11... | collective-permute-start | bytes 110600 | tf_op jit(solution)/shard_map/cond/branch_1_fun/ppermute | solution.py:36
  41.1 2.6 %collective-permute-done.9 = f16[3,3,2048]{2,1,0:T(4,128)(2,1)S(1)} collective-permute-done((f16[3,3,2048]{2,1,0:T(4,128)(2,1)S(1)}, f16[3,3,2048]{2,1,0:T(4,128)(2,1)S(1)}, u32[]{:S(2)}, u32[]{:S(2)}) %collective-permute-start.9) | collective-permute-done | bytes 36896 | tf_op jit(solution)/shard_map/cond/branch_1_fun/ppermute | solution.py:36
  44.0 3.0 %branch_1_fun.3 = f32[3,64,2048]{2,1,0:T(8,128)S(1)} custom-call(s32[1]{0:T(128)} %bitcast.14.where_ref, f32[3,80,2048]{2,1,0:T(8,128)S(1)} %fusion.3.state_ref, f32[80,2048]{1,0:T(8,128)S(1)} %fusion.8.depth_ref, f32[2,2,80,2048]{3,2,1,0:T(8,128)S(1)} %branch_1_fun.2.wind_ref), custom_call_target="tpu_custom_call" | custom-call | flops 49152000 | bytes 7864320 | tf_op jit(solution)/shard_map/cond/branch_1_fun/pallas_call | solution.py:193
  47.2 1.1 %copy-done.2 = f32[1,3,64,2048]{3,2,1,0:T(8,128)} copy-done((f32[1,3,64,2048]{3,2,1,0:T(8,128)}, f32[1,3,64,2048]{3,2,1,0:T(8,128)S(1)}, u32[]{:S(2)}) %copy-start.2) | copy-done | bytes 1572888
  (33 shorter events, 2.7 us)
Async XLA Ops:
  3.8 1.9 %collective-permute-start = (f16[3,32,2048]{2,1,0:T(8,128)(2,1)S(1)}, f16[3,32,2048]{2,1,0:T(8,128)(2,1)S(1)}, u32[]{:S(2)}, u32[]{:S(2)}) collective-permute-start(f16[3,32,2048]{2,1,0:T(8,128)(2,1)S(1)} %get-tuple-element.99), channel_id=1, source_target_pairs={{0,2},{2,0},{4,6},{6,4},{8,10},{10,8},{12,14},{14,12},{16,18},{18,... | collective-permute-start | bytes 1179656 | tf_op jit(solution)/shard_map/cond/branch_1_fun/ppermute | solution.py:237
  5.8 6.6 %copy-start.1 = (f32[64,2048]{1,0:T(8,128)S(1)}, f32[64,2048]{1,0:T(8,128)}, u32[]{:S(2)}) copy-start(f32[64,2048]{1,0:T(8,128)} %get-tuple-element.47) | copy-start | bytes 1572868 | tf_op jit(solution)/shard_map/cond
  6.0 13.6 %collective-permute-start.2 = (f16[2,3,32,2048]{3,2,1,0:T(8,128)(2,1)S(1)}, f16[2,3,32,2048]{3,2,1,0:T(8,128)(2,1)S(1)}, u32[]{:S(2)}, u32[]{:S(2)}) collective-permute-start(f16[2,3,32,2048]{3,2,1,0:T(8,128)(2,1)S(1)} %select_convert_fusion.2), channel_id=1, source_target_pairs={{10,18},{14,22},{18,10},{22,14},{11,19},{15,23},{19,11},{23,15}} | collective-permute-start | bytes 2359304 | tf_op jit(solution)/shard_map/cond/branch_1_fun/ppermute | solution.py:237
  6.7 12.9 %collective-permute-start.1 = (f16[2,3,32,2048]{3,2,1,0:T(8,128)(2,1)S(1)}, f16[2,3,32,2048]{3,2,1,0:T(8,128)(2,1)S(1)}, u32[]{:S(2)}, u32[]{:S(2)}) collective-permute-start(f16[2,3,32,2048]{3,2,1,0:T(8,128)(2,1)S(1)} %select_convert_fusion.2), channel_id=1, source_target_pairs={{0,4},{4,0},{8,12},{12,8},{16,20},{20,16},{24,28},{28,24},{2,10},{... | collective-permute-start | bytes 2359304 | tf_op jit(solution)/shard_map/cond/branch_1_fun/ppermute | solution.py:237
  10.8 5.6 %collective-permute-start.3 = (bf16[80,1024]{1,0:T(8,128)(2,1)S(1)}, bf16[80,1024]{1,0:T(8,128)(2,1)S(1)}, u32[]{:S(2)}, u32[]{:S(2)}) collective-permute-start(bf16[80,1024]{1,0:T(8,128)(2,1)S(1)} %bitcast.62), channel_id=1, source_target_pairs={{0,1},{1,0},{2,3},{3,2},{4,5},{5,4},{6,7},{7,6},{8,9},{9,8},{10,11... | collective-permute-start | bytes 491528 | tf_op jit(solution)/shard_map/cond/branch_1_fun/ppermute | solution.py:64
  12.4 6.1 %collective-permute-start.5 = (f32[3,2048]{1,0:T(4,128)S(1)}, f32[3,2048]{1,0:T(4,128)S(1)}, u32[]{:S(2)}, u32[]{:S(2)}) collective-permute-start(f32[3,2048]{1,0:T(4,128)S(1)} %slice_select_fusion.1), channel_id=1, source_target_pairs={{0,1},{1,0},{2,3},{3,2},{4,5},{5,4},{6,7},{7,6},{8,9},{9,8},{10,11... | collective-permute-start | bytes 73736 | tf_op jit(solution)/shard_map/cond/branch_1_fun/ppermute | solution.py:36
  16.5 3.1 %collective-permute-start.4 = (bf16[80,1024]{1,0:T(8,128)(2,1)S(1)}, bf16[80,1024]{1,0:T(8,128)(2,1)S(1)}, u32[]{:S(2)}, u32[]{:S(2)}) collective-permute-start(bf16[80,1024]{1,0:T(8,128)(2,1)S(1)} %bitcast_select_fusion), channel_id=1, source_target_pairs={{0,2},{2,0},{4,6},{6,4},{8,10},{10,8},{12,14},{14,12},{16,18},{18,... | collective-permute-start | bytes 491528 | tf_op jit(solution)/shard_map/cond/branch_1_fun/ppermute | solution.py:75
  20.8 8.1 %collective-permute-start.7 = (f16[2,3,32,2048]{3,2,1,0:T(8,128)(2,1)S(1)}, f16[2,3,32,2048]{3,2,1,0:T(8,128)(2,1)S(1)}, u32[]{:S(2)}, u32[]{:S(2)}) collective-permute-start(f16[2,3,32,2048]{3,2,1,0:T(8,128)(2,1)S(1)} %get-tuple-element.96), channel_id=1, source_target_pairs={{8,16},{12,20},{16,8},{20,12},{9,17},{13,21},{17,9},{21,13}} | collective-permute-start | bytes 2359304 | tf_op jit(solution)/shard_map/cond/branch_1_fun/ppermute | solution.py:237
  21.7 14.9 %collective-permute-start.6 = (f16[2,3,32,2048]{3,2,1,0:T(8,128)(2,1)S(1)}, f16[2,3,32,2048]{3,2,1,0:T(8,128)(2,1)S(1)}, u32[]{:S(2)}, u32[]{:S(2)}) collective-permute-start(f16[2,3,32,2048]{3,2,1,0:T(8,128)(2,1)S(1)} %get-tuple-element.97), channel_id=1, source_target_pairs={{0,8},{4,12},{16,24},{20,28},{8,0},{12,4},{24,16},{28,20},{2,6},{6... | collective-permute-start | bytes 2359304 | tf_op jit(solution)/shard_map/cond/branch_1_fun/ppermute | solution.py:237
  37.3 1.8 %collective-permute-start.8 = (f16[3,32,2048]{2,1,0:T(8,128)(2,1)S(1)}, f16[3,32,2048]{2,1,0:T(8,128)(2,1)S(1)}, u32[]{:S(2)}, u32[]{:S(2)}) collective-permute-start(f16[3,32,2048]{2,1,0:T(8,128)(2,1)S(1)} %fusion.9), channel_id=1, source_target_pairs={{0,2},{2,0},{4,6},{6,4},{8,10},{10,8},{12,14},{14,12},{16,18},{18,... | collective-permute-start | bytes 1179656 | tf_op jit(solution)/shard_map/cond/branch_1_fun/ppermute | solution.py:237
  39.5 4.2 %collective-permute-start.9 = (f16[3,3,2048]{2,1,0:T(4,128)(2,1)S(1)}, f16[3,3,2048]{2,1,0:T(4,128)(2,1)S(1)}, u32[]{:S(2)}, u32[]{:S(2)}) collective-permute-start(f16[3,3,2048]{2,1,0:T(4,128)(2,1)S(1)} %slice_select_fusion), channel_id=1, source_target_pairs={{0,1},{1,0},{2,3},{3,2},{4,5},{5,4},{6,7},{7,6},{8,9},{9,8},{10,11... | collective-permute-start | bytes 110600 | tf_op jit(solution)/shard_map/cond/branch_1_fun/ppermute | solution.py:36
  47.2 1.1 %copy-start.2 = (f32[1,3,64,2048]{3,2,1,0:T(8,128)}, f32[1,3,64,2048]{3,2,1,0:T(8,128)S(1)}, u32[]{:S(2)}) copy-start(f32[1,3,64,2048]{3,2,1,0:T(8,128)S(1)} %get-tuple-element.132) | copy-start | bytes 4718596

commit v3 on v2

--- a/solution.py
+++ b/solution.py
@@ -11,15 +11,23 @@
 TIME_STEP = 0.4
 EDGE = 3
 PAD = 8
-VMEM_BYTES = 48 * 1024 * 1024
-CHUNKS = 1
-
-
-def parent_list(offspring):
+WIND_VMEM = 10 * 1024 * 1024
+STEP_VMEM = 20 * 1024 * 1024
+CHUNKS = 2
+
+
+def parents_by_starts(offspring):
+    running = jnp.cumsum(offspring)
+    return lambda slots: jnp.sum((running[None, :] <= slots[:, None]).astype(jnp.int32), axis=1)
+
+
+def parents_by_ends(offspring):
     count = offspring.shape[0]
-    running = jnp.cumsum(offspring)
-    slots = jnp.arange(count, dtype=jnp.int32)
-    return jnp.sum((running[None, :] <= slots[:, None]).astype(jnp.int32), axis=1)
+    index = jnp.arange(count)
+    running = jnp.sum(jnp.where(index[None, :] <= index[:, None], offspring[None, :], 0), axis=1)
+    return lambda slots: count - jnp.sum(
+        (running[None, :] > slots[:, None]).astype(jnp.int32), axis=1
+    )
 
 
 def swap_edges(head, tail):
@@ -70,11 +78,19 @@
         return found
 
     if not shared:
-        return jnp.concatenate([fetch(start_hour[0]), fetch(start_hour[0] + 1)]), first_row(me)
-    found = fetch(start_hour[0] + odd)
-    other = lax.ppermute(found, "dom", [(i, i ^ 1) for i in range(devices)])
-    both = [jnp.where(odd == 0, found, other), jnp.where(odd == 0, other, found)]
-    return jnp.concatenate(both), first_row(me)
+        return [fetch(start_hour[0]), fetch(start_hour[0] + 1)], first_row(me)
+    return [fetch(start_hour[0] + odd)], first_row(me)
+
+
+def both_hours(panels):
+    if len(panels) == 2:
+        return jnp.concatenate(panels)
+    odd = lax.axis_index("dom") % 2
+    found = panels[0]
+    other = lax.ppermute(found, "dom", [(i, i ^ 1) for i in range(lax.axis_size("dom"))])
+    return jnp.concatenate(
+        [jnp.where(odd == 0, found, other), jnp.where(odd == 0, other, found)]
+    )
 
 
 def wind_kernel(where_ref, coarse_ref, fine_ref):
@@ -112,7 +128,7 @@
             pl.BlockSpec(memory_space=pltpu.VMEM),
         ],
         out_specs=pl.BlockSpec(memory_space=pltpu.VMEM),
-        compiler_params=pltpu.CompilerParams(vmem_limit_bytes=VMEM_BYTES),
+        compiler_params=pltpu.CompilerParams(vmem_limit_bytes=WIND_VMEM),
         cost_estimate=pl.CostEstimate(
             flops=4 * hours * parts * rows * window * cols,
             bytes_accessed=8 * hours * parts * rows * cols,
@@ -200,7 +216,7 @@
             pltpu.VMEM((parts, rows, cols), jnp.float32),
             pltpu.VMEM((1, rows, cols), jnp.float32),
         ],
-        compiler_params=pltpu.CompilerParams(vmem_limit_bytes=VMEM_BYTES),
+        compiler_params=pltpu.CompilerParams(vmem_limit_bytes=STEP_VMEM),
         cost_estimate=pl.CostEstimate(
             flops=100 * parts * rows * cols,
             bytes_accessed=4 * (3 * parts + 3) * rows * cols,
@@ -219,8 +235,17 @@
     return array.astype(jnp.float32)
 
 
-def unit_of(pool, unit):
-    return jnp.where(unit == 0, wide(pool[0])[None], wide(pool[1])[None])
+def picked(pools, code):
+    units = [pool[unit] for pool in pools for unit in range(2)]
+    result = wide(units[0])[None]
+    for at, unit in enumerate(units[1:], 1):
+        result = jnp.where(code == at, wide(unit)[None], result)
+    return result
+
+
+def once(cells, array):
+    row = wide(cells[0, 0, :1, : array.shape[-1]])
+    return jnp.where(jnp.abs(row) > 1e30, jnp.zeros_like(array), array)
 
 
 class Near:
@@ -265,43 +290,38 @@
         two = self.move(mine, self.along(1, 1))
         return mine, one, two
 
-    def held(self, pools, parent):
-        mine, one, two = lax.optimization_barrier(pools)
-        unit = parent % 2
+    def held(self, parent):
         place = parent // 4
         in_one = jnp.where(self.first, parent // 2 % 2 != self.pair, place == self.even_group)
         in_two = ~self.first & (place == self.odd_group) & ~in_one
-        rest = jnp.where(in_one, unit_of(one, unit), unit_of(mine, unit))
-        return jnp.where(in_two, unit_of(two, unit), rest)
-
-    def wanted(self, parents, to_group, to_pair):
-        base = 4 * jnp.clip(to_group, 0, self.groups - 1) + 2 * to_pair
-        return lax.dynamic_slice_in_dim(parents, base, 2).reshape(2, 1, 1, 1)
-
-    def second_round(self, pools, parents):
-        first, pair = self.first, self.pair
-        to_even = self.wanted(
-            parents,
-            jnp.where(first, self.even_group, self.group),
-            jnp.where(first, pair, 1 - pair),
-        )
-        to_odd = self.wanted(parents, self.odd_group, pair)
-        send = self.held(pools, to_even).astype(jnp.float16)
-        three = self.move(send, self.along(0, 0) + self.across(1))
-        send = self.held(pools, to_odd).astype(jnp.float16)
-        four = self.move(send, self.along(0, 1))
-        return three, four
-
-    def slots(self, pools, three, four, parents):
-        first = self.first
-        parent = self.wanted(parents, self.group, self.pair)
+        return parent % 2 + jnp.where(in_two, 4, jnp.where(in_one, 2, 0))
+
+    def codes(self, parents_of):
+        first, pair, group = self.first, self.pair, self.group
+        entry = jnp.arange(6)
+        kind, unit = entry // 2, entry % 2
+        unit = jnp.where(kind == 2, unit ^ self.core, unit)
+        to_group = jnp.where(kind == 0, jnp.where(first, self.even_group, group), group)
+        to_group = jnp.where(kind == 1, self.odd_group, to_group)
+        to_pair = jnp.where((kind == 0) & ~first, 1 - pair, pair)
+        parent = parents_of(4 * jnp.clip(to_group, 0, self.groups - 1) + 2 * to_pair + unit)
         place = parent // 4
-        in_three = jnp.where(first, place == self.even_group, parent // 2 % 2 != self.pair)
-        in_four = first & (place == self.odd_group) & (place != self.group) & ~in_three
-        both = jnp.where(in_three, wide(three), self.held(pools, parent))
-        both = jnp.where(in_four, wide(four), both)
-        own = jnp.where(first, both[0], both[1]).astype(jnp.float16)
-        return own, jnp.where(first, both[1], both[0]).astype(jnp.float16)
+        in_three = jnp.where(first, place == self.even_group, parent // 2 % 2 != pair)
+        in_four = first & (place == self.odd_group) & (place != group) & ~in_three
+        here = jnp.where(in_three, 6 + unit, jnp.where(in_four, 8 + unit, self.held(parent)))
+        code = jnp.where(kind == 2, here, self.held(parent)).reshape(-1, 1, 1, 1)
+        return code[:2], code[2:4], code[4:]
+
+    def to_send(self, pools, codes):
+        return [picked(pools, code) for code in codes[:2]]
+
+    def second_round(self, even, odd):
+        three = self.move(even, self.along(0, 0) + self.across(1))
+        return three, self.move(odd, self.along(0, 1))
+
+    def slots(self, pools, codes):
+        both = picked(pools, codes[2]).astype(jnp.float16)
+        return both[0], both[1]
 
 
 def body(states, offspring, sea_depth, wind, start_hour):
@@ -310,14 +330,13 @@
     first = lax.axis_index("tile") * row_count - PAD
     rows = row_count + 2 * PAD
     fill = ((PAD - EDGE, 0), (0, 0)), ((0, PAD - EDGE), (0, 0))
-    parents = parent_list(offspring)
-    slots = jnp.arange(parents.shape[0], dtype=jnp.int32)
+    slots = jnp.arange(offspring.shape[0], dtype=jnp.int32)
+    parents = parents_by_starts(offspring)(slots)
     state = states[0]
 
     def surroundings(sea_depth, wind):
-        coarse, base = wind_window(wind, start_hour, row_count)
-        above, below = swap_edges(sea_depth[:EDGE], sea_depth[-EDGE:])
-        return coarse, base, above, below
+        panels, base = wind_window(wind, start_hour, row_count)
+        return panels, base, *swap_edges(sea_depth[:EDGE], sea_depth[-EDGE:])
 
     def fields(sea_depth, coarse, base, above, below):
         depth = (0.5 * TIME_STEP) * jnp.concatenate(
@@ -333,34 +352,44 @@
         return step(jnp.concatenate(pieces, axis=1), depth, stress, first, total_rows)
 
     def far():
-        around = surroundings(sea_depth, wind)
+        panels, *edges = surroundings(sea_depth, wind)
         copied = exchange_all(state.astype(jnp.float16), parents)
-        return finish([copied], *fields(sea_depth, *around))
+        return finish([copied], *fields(sea_depth, both_hours(panels), *edges))
 
     def near():
         plan = Near()
-        keep, send = plan.halves(state)
+        after = lax.optimization_barrier
+        keep, send = after(plan.halves(state))
         got = plan.move(send, plan.neighbour())
         size = keep.shape[1] // CHUNKS
         pools = [
             plan.first_round(plan.pair_halves(keep[:, at : at + size], got[:, at : at + size]))
             for at in range(0, CHUNKS * size, size)
         ]
-        mine, later_depth, later_wind = lax.optimization_barrier(
-            ([pool[0] for pool in pools], sea_depth, wind)
+        mine, near_depth, near_wind, near_offspring = after(
+            ([pool[0] for pool in pools], sea_depth, wind, offspring)
         )
         pools = [(own,) + pool[1:] for own, pool in zip(mine, pools)]
-        around = surroundings(later_depth, later_wind)
-        pools[-1], around = lax.optimization_barrier((pools[-1], around))
-        moved = [plan.second_round(pool, parents) for pool in pools]
-        depth, stress = fields(sea_depth, *around)
-        moved[-1], depth, stress = lax.optimization_barrier((moved[-1], depth, stress))
+        panels, *edges = surroundings(near_depth, near_wind)
+        moved, ready = [None] * CHUNKS, None
+        codes = [plan.codes(ways(near_offspring)) for ways in (parents_by_starts, parents_by_ends)]
+        for at in reversed(range(CHUNKS)):
+            sends = plan.to_send(pools[at], codes[at % 2])
+            if ready:
+                sends = [once(cells, send) for cells, send in zip(ready, sends)]
+            ready = [send.astype(jnp.float16) for send in sends]
+            moved[at] = plan.second_round(*ready)
+        panels = [once(ready[1], panel) for panel in panels]
+        edges[1:] = [once(ready[1], edge) for edge in edges[1:]]
+        coarse = both_hours(panels)
+        depth, stress = fields(near_depth, coarse, *edges)
+        moved[0], depth, stress = after((moved[0], depth, stress))
         upper, lower = [], []
-        for pool, (three, four) in zip(pools, moved):
-            own, other = plan.slots(pool, three, four, parents)
-            other = plan.move(other, plan.neighbour())
-            upper.append(jnp.where(plan.first, wide(own), wide(other)).astype(jnp.float16))
-            lower.append(jnp.where(plan.first, wide(other), wide(own)).astype(jnp.float16))
+        for at in range(CHUNKS):
+            own, other = plan.slots(pools[at] + moved[at], codes[at % 2])
+            got = plan.move(other, plan.neighbour())
+            upper.append(jnp.where(plan.first, wide(own), wide(got)).astype(jnp.float16))
+            lower.append(jnp.where(plan.first, wide(got), wide(own)).astype(jnp.float16))
         return finish(upper + lower, depth, stress)
 
     if parents.shape[0] % 4 or row_count % (2 * CHUNKS):

time: 48.6 us -> 44.6 us (0.918)
  waiting for transfers between devices: 16.9 us -> 7.96 us
  starting transfers between devices: 15.8 us -> 18.8 us
  other arithmetic: 5.68 us -> 6.75 us
    ppermute x6 -> x11, waiting for transfers between devices: 9.86 us -> 5.36 us  [move(): return lax.ppermute(array, 'dom', pairs) if pairs else array]
    ppermute x1, waiting for transfers between devices: 3.47 us -> 0.01 us  [fetch(): lax.ppermute(panel(hour, (me + shift) % count), 'tile', [(i, (i + shift)...]
    ppermute x6 -> x11, starting transfers between devices: 10.1 us -> 13.1 us  [move(): return lax.ppermute(array, 'dom', pairs) if pairs else array]
    convert_element_type x4 -> x7, other arithmetic: 1.15 us -> 3.52 us  [the longest x1 1.48 us: halves(): return (keep, send.astype(jnp.float16))]
    ppermute x1, starting transfers between devices: 2.03 us -> 0.07 us  [both_hours(): lax.ppermute(found, 'dom', [(i, i ^ 1) for i in range(lax.axis_size('dom'...]
    dynamic_slice x1 -> x0, other arithmetic: 1.48 us -> none  [halves(): keep = lax.dynamic_slice_in_dim(state, self.core * half, half, 1)]
    ppermute x2, starting transfers between devices: 2.16 us -> 3.59 us  [swap_edges(): got = lax.ppermute(jnp.where(upper, tail, head), 'tile', pairs)]
    ppermute x1, waiting for transfers between devices: 1.01 us -> 0.01 us  [both_hours(): lax.ppermute(found, 'dom', [(i, i ^ 1) for i in range(lax.axis_size('dom'...]
  transfers between devices with their start and end apart: 10 -> 15, of which waited for: 7 -> 6; matrix products, arithmetic and copies ran while one was open for 3% -> 11% of each run, Pallas kernels for 4% -> 5%
where the time goes in v3:
time: 44.6 us; the launch traced here: 44.4 us
  starting transfers between devices  18.8 us (42%)
  waiting for transfers between devices  7.96 us (18%)
  other arithmetic  6.75 us (15%)
  Pallas kernels  5.36 us (12%)
  local copies, waits for them, and re-layouts  3.34 us (7%)
  loops' own time  1.49 us (3%)
  between operations  0.67 us (2%)
    ppermute x11, starting transfers between devices, move(): return lax.ppermute(array, 'dom', pairs) if pairs else array  13.1 us
    ppermute x11, waiting for transfers between devices, move(): return lax.ppermute(array, 'dom', pairs) if pairs else array  5.36 us
    ppermute x2, starting transfers between devices, swap_edges(): got = lax.ppermute(jnp.where(upper, tail, head), 'tile', pairs)  3.59 us
    pallas_call x1, Pallas kernels, step(): pl.pallas_call(functools.partial(step_kernel, total_rows), out_shape=jax....  3.24 us
    ppermute x2, waiting for transfers between devices, swap_edges(): got = lax.ppermute(jnp.where(upper, tail, head), 'tile', pairs)  2.6 us
    pallas_call x1, Pallas kernels, fine_wind(): pl.pallas_call(wind_kernel, out_shape=jax.ShapeDtypeStruct((hours, parts,...  2.12 us
    ppermute x1, starting transfers between devices, fetch(): lax.ppermute(panel(hour, (me + shift) % count), 'tile', [(i, (i + shift)...  1.99 us
    another operation x1, loops' own time, body(): return lax.cond(close, near, far)[None]  1.49 us
  transfers between devices with their start and end apart: 15, of which 6 were waited for; matrix products, arithmetic and copies ran while one was open for 11% of the time, Pallas kernels for 5%

profile of v3, /device:TPU:0, one launch (start us, length us, event | category | flops | bytes accessed | tf_op | source)
XLA Modules:
  0.0 44.4 jit_solution(10447953823772961988)
XLA Ops:
  0.0 0.7 %copy.27 = s32[16,1]{1,0:T(8,128)S(1)} copy(s32[16,1]{0,1:T(1,128)} %bitcast.144) | data formatting | bytes 128 | tf_op jit(solution)/shard_map/reshape.211
  1.0 0.7 %compare_reduce_fusion.4 = pred[]{:T(512)} fusion(s32[16]{0:T(128)S(1)} %convert_reduce_fusion.2), kind=kLoop, calls=%fused_computation.220 | loop fusion | flops 431 | bytes 65 | tf_op jit(solution)/shard_map/reduce_and | solution.py:397
  2.3 40.9 %conditional.1 = (f32[1,3,64,2048]{3,2,1,0:T(8,128)S(1)}) conditional(s32[]{:T(128)} %convert_element_type.201, (s32[]{:T(128)}, s32[16]{0:T(128)S(1)}, f32[3,64,2048]{2,1,0:T(8,128)}, f32[64,2048]{1,0:T(8,128)}, s32[1]{0:T(128)}, /*index=5*/bf16[3,2,64,1024]{3,2,1,0:T(8,128)(2,1)}) %tuple.86, (s32[]{:T(128)}, f32[3,64,2048]{2,1,0:T(8,128)}, ...), branch_computations={%region_3.4_spmd, %region_4.9_spmd} | conditional | flops 118075048 | bytes 75721944 | solution.py:398
  2.4 1.5 %dynamic-slice_convert_fusion = (f16[3,32,2048]{2,1,0:T(8,128)(2,1)S(1)}, f32[3,32,2048]{2,1,0:T(8,128)S(1)}) fusion(f32[3,64,2048]{2,1,0:T(8,128)} %get-tuple-element.40, s32[]{:T(128)S(6)} %select_n.439, s32[]{:T(128)S(6)} %select_n.438), kind=kLoop, calls=%fused_computation.38 | loop fusion | flops 196608 | bytes 2752520 | tf_op jit(solution)/shard_map/cond/branch_1_fun/convert_element_type | solution.py:282
  3.8 0.5 %collective-permute-start = (f16[3,32,2048]{2,1,0:T(8,128)(2,1)S(1)}, f16[3,32,2048]{2,1,0:T(8,128)(2,1)S(1)}, u32[]{:S(2)}, u32[]{:S(2)}) collective-permute-start(f16[3,32,2048]{2,1,0:T(8,128)(2,1)S(1)} %get-tuple-element.42), channel_id=1, source_target_pairs={{0,2},{2,0},{4,6},{6,4},{8,10},{10,8},{12,14},{14,12},{16,18},{18,... | collective-permute-start | bytes 1179656 | tf_op jit(solution)/shard_map/cond/branch_1_fun/ppermute | solution.py:262
  6.0 3.0 %collective-permute-start.2 = (f16[2,3,16,2048]{3,2,1,0:T(8,128)(2,1)S(1)}, f16[2,3,16,2048]{3,2,1,0:T(8,128)(2,1)S(1)}, u32[]{:S(2)}, u32[]{:S(2)}) collective-permute-start(f16[2,3,16,2048]{3,2,1,0:T(8,128)(2,1)S(1)} %get-tuple-element.47), channel_id=1, source_target_pairs={{0,4},{4,0},{8,12},{12,8},{16,20},{20,16},{24,28},{28,24},{2,10},{... | collective-permute-start | bytes 1179656 | tf_op jit(solution)/shard_map/cond/branch_1_fun/ppermute | solution.py:262
  8.9 0.7 %collective-permute-start.1 = (f16[2,3,16,2048]{3,2,1,0:T(8,128)(2,1)S(1)}, f16[2,3,16,2048]{3,2,1,0:T(8,128)(2,1)S(1)}, u32[]{:S(2)}, u32[]{:S(2)}) collective-permute-start(f16[2,3,16,2048]{3,2,1,0:T(8,128)(2,1)S(1)} %get-tuple-element.47), channel_id=1, source_target_pairs={{10,18},{14,22},{18,10},{22,14},{11,19},{15,23},{19,11},{23,15}} | collective-permute-start | bytes 1179656 | tf_op jit(solution)/shard_map/cond/branch_1_fun/ppermute | solution.py:262
  9.7 0.7 %collective-permute-start.6 = (f16[2,3,16,2048]{3,2,1,0:T(8,128)(2,1)S(1)}, f16[2,3,16,2048]{3,2,1,0:T(8,128)(2,1)S(1)}, u32[]{:S(2)}, u32[]{:S(2)}) collective-permute-start(f16[2,3,16,2048]{3,2,1,0:T(8,128)(2,1)S(1)} %get-tuple-element.48), channel_id=1, source_target_pairs={{10,18},{14,22},{18,10},{22,14},{11,19},{15,23},{19,11},{23,15}} | collective-permute-start | bytes 1179656 | tf_op jit(solution)/shard_map/cond/branch_1_fun/ppermute | solution.py:262
  11.2 2.0 %collective-permute-start.10 = (f32[3,2048]{1,0:T(4,128)S(1)}, f32[3,2048]{1,0:T(4,128)S(1)}, u32[]{:S(2)}, u32[]{:S(2)}) collective-permute-start(f32[3,2048]{1,0:T(4,128)S(1)} %slice_select_fusion.3), channel_id=1, source_target_pairs={{0,1},{1,0},{2,3},{3,2},{4,5},{5,4},{6,7},{7,6},{8,9},{9,8},{10,11... | collective-permute-start | bytes 73736 | tf_op jit(solution)/shard_map/cond/branch_1_fun/ppermute | solution.py:44
  13.3 1.1 %constant_dynamic-slice_fusion.2 = (bf16[1,2,40,1024]{3,2,1,0:T(8,128)(2,1)S(1)}, bf16[1,2,40,1024]{3,2,1,0:T(8,128)(2,1)S(1)}) fusion(bf16[3,2,64,1024]{3,2,1,0:T(8,128)(2,1)} %get-tuple-element.51, s32[]{:T(128)S(6)} %select_n.523, s32[]{:T(128)} %min.23, s32[]{:T(128)S(6)} %min.24), kind=kLoop, calls=%fused_computation.151 | loop fusion | bytes 655372 | tf_op jit(solution)/shard_map/cond/branch_1_fun/dynamic_slice | solution.py:64
  14.7 2.0 %collective-permute-start.11 = (bf16[80,1024]{1,0:T(8,128)(2,1)S(1)}, bf16[80,1024]{1,0:T(8,128)(2,1)S(1)}, u32[]{:S(2)}, u32[]{:S(2)}) collective-permute-start(bf16[80,1024]{1,0:T(8,128)(2,1)S(1)} %bitcast.142), channel_id=1, source_target_pairs={{0,1},{1,0},{2,3},{3,2},{4,5},{5,4},{6,7},{7,6},{8,9},{9,8},{10,11... | collective-permute-start | bytes 491528 | tf_op jit(solution)/shard_map/cond/branch_1_fun/ppermute | solution.py:72
  17.3 0.9 %collective-permute-start.3 = (f16[2,3,16,2048]{3,2,1,0:T(8,128)(2,1)S(1)}, f16[2,3,16,2048]{3,2,1,0:T(8,128)(2,1)S(1)}, u32[]{:S(2)}, u32[]{:S(2)}) collective-permute-start(f16[2,3,16,2048]{3,2,1,0:T(8,128)(2,1)S(1)} %get-tuple-element.81), channel_id=1, source_target_pairs={{8,16},{12,20},{16,8},{20,12},{9,17},{13,21},{17,9},{21,13}} | collective-permute-start | bytes 1179656 | tf_op jit(solution)/shard_map/cond/branch_1_fun/ppermute | solution.py:262
  18.3 0.7 %collective-permute-done.7 = f16[2,3,16,2048]{3,2,1,0:T(8,128)(2,1)S(1)} collective-permute-done((f16[2,3,16,2048]{3,2,1,0:T(8,128)(2,1)S(1)}, f16[2,3,16,2048]{3,2,1,0:T(8,128)(2,1)S(1)}, u32[]{:S(2)}, u32[]{:S(2)}) %collective-permute-start.7) | collective-permute-done | bytes 393248 | tf_op jit(solution)/shard_map/cond/branch_1_fun/ppermute | solution.py:262
  18.9 3.8 %collective-permute-start.4 = (f16[2,3,16,2048]{3,2,1,0:T(8,128)(2,1)S(1)}, f16[2,3,16,2048]{3,2,1,0:T(8,128)(2,1)S(1)}, u32[]{:S(2)}, u32[]{:S(2)}) collective-permute-start(f16[2,3,16,2048]{3,2,1,0:T(8,128)(2,1)S(1)} %get-tuple-element.82), channel_id=1, source_target_pairs={{0,8},{4,12},{16,24},{20,28},{8,0},{12,4},{24,16},{28,20},{2,6},{6... | collective-permute-start | bytes 1179656 | tf_op jit(solution)/shard_map/cond/branch_1_fun/ppermute | solution.py:262
  22.8 0.6 %select_convert_fusion.1 = (f16[2,3,16,2048]{3,2,1,0:T(8,128)(2,1)S(1)}, f16[2,3,16,2048]{3,2,1,0:T(8,128)(2,1)S(1)}) fusion(f32[3,16,2048]{2,1,0:T(8,128)S(1)} %get-tuple-element.108, f32[3,16,2048]{2,1,0:T(8,128)S(1)} %get-tuple-element.107, f32[3,16,2048]{2,1,0:T(8,128)S(1)} %get-tuple-element.106, f32[3,16,2048]{2,1,0:T(8,128)S(1)} %get-tuple-element.105, ...), kind=kLoop, calls=%fused_computation.31 | loop fusion | flops 2752512 | bytes 3149844 | tf_op jit(solution)/shard_map/cond/branch_1_fun/convert_element_type | solution.py:380
  23.5 0.7 %collective-permute-start.9 = (f16[2,3,16,2048]{3,2,1,0:T(8,128)(2,1)S(1)}, f16[2,3,16,2048]{3,2,1,0:T(8,128)(2,1)S(1)}, u32[]{:S(2)}, u32[]{:S(2)}) collective-permute-start(f16[2,3,16,2048]{3,2,1,0:T(8,128)(2,1)S(1)} %get-tuple-element.79), channel_id=1, source_target_pairs={{8,16},{12,20},{16,8},{20,12},{9,17},{13,21},{17,9},{21,13}} | collective-permute-start | bytes 1179656 | tf_op jit(solution)/shard_map/cond/branch_1_fun/ppermute | solution.py:262
  24.3 2.7 %collective-permute-start.8 = (f16[2,3,16,2048]{3,2,1,0:T(8,128)(2,1)S(1)}, f16[2,3,16,2048]{3,2,1,0:T(8,128)(2,1)S(1)}, u32[]{:S(2)}, u32[]{:S(2)}) collective-permute-start(f16[2,3,16,2048]{3,2,1,0:T(8,128)(2,1)S(1)} %get-tuple-element.80), channel_id=1, source_target_pairs={{0,8},{4,12},{16,24},{20,28},{8,0},{12,4},{24,16},{28,20},{2,6},{6... | collective-permute-start | bytes 1179656 | tf_op jit(solution)/shard_map/cond/branch_1_fun/ppermute | solution.py:262
  27.2 2.1 %branch_1_fun.2.wind_ref = f32[2,2,80,2048]{3,2,1,0:T(8,128)S(1)} custom-call(s32[2]{0:T(128)S(1)} %pad_add_fusion.1.where_ref, bf16[160,1024]{1,0:T(8,128)(2,1)S(1)} %pad_maximum_fusion.1.coarse_ref), custom_call_target="tpu_custom_call" | custom-call | flops 52428800 | bytes 2621440 | tf_op jit(solution)/shard_map/cond/branch_1_fun/pallas_call | solution.py:123
  30.1 2.7 %collective-permute-done.8 = f16[2,3,16,2048]{3,2,1,0:T(8,128)(2,1)S(1)} collective-permute-done((f16[2,3,16,2048]{3,2,1,0:T(8,128)(2,1)S(1)}, f16[2,3,16,2048]{3,2,1,0:T(8,128)(2,1)S(1)}, u32[]{:S(2)}, u32[]{:S(2)}) %collective-permute-start.8) | collective-permute-done | bytes 393248 | tf_op jit(solution)/shard_map/cond/branch_1_fun/ppermute | solution.py:262
  33.6 1.3 %collective-permute-done.13 = f16[3,16,2048]{2,1,0:T(8,128)(2,1)S(1)} collective-permute-done((f16[3,16,2048]{2,1,0:T(8,128)(2,1)S(1)}, f16[3,16,2048]{2,1,0:T(8,128)(2,1)S(1)}, u32[]{:S(2)}, u32[]{:S(2)}) %collective-permute-start.13) | collective-permute-done | bytes 196640 | tf_op jit(solution)/shard_map/cond/branch_1_fun/ppermute | solution.py:262
  35.1 1.6 %collective-permute-start.14 = (f16[3,3,2048]{2,1,0:T(4,128)(2,1)S(1)}, f16[3,3,2048]{2,1,0:T(4,128)(2,1)S(1)}, u32[]{:S(2)}, u32[]{:S(2)}) collective-permute-start(f16[3,3,2048]{2,1,0:T(4,128)(2,1)S(1)} %slice_select_fusion.2), channel_id=1, source_target_pairs={{0,1},{1,0},{2,3},{3,2},{4,5},{5,4},{6,7},{7,6},{8,9},{9,8},{10,11... | collective-permute-start | bytes 110600 | tf_op jit(solution)/shard_map/cond/branch_1_fun/ppermute | solution.py:44
  36.6 2.6 %collective-permute-done.14 = f16[3,3,2048]{2,1,0:T(4,128)(2,1)S(1)} collective-permute-done((f16[3,3,2048]{2,1,0:T(4,128)(2,1)S(1)}, f16[3,3,2048]{2,1,0:T(4,128)(2,1)S(1)}, u32[]{:S(2)}, u32[]{:S(2)}) %collective-permute-start.14) | collective-permute-done | bytes 36896 | tf_op jit(solution)/shard_map/cond/branch_1_fun/ppermute | solution.py:44
  39.7 3.2 %branch_1_fun.3 = f32[3,64,2048]{2,1,0:T(8,128)S(1)} custom-call(s32[1]{0:T(128)} %bitcast.14.where_ref, f32[3,80,2048]{2,1,0:T(8,128)S(1)} %concatenate.21.state_ref, f32[80,2048]{1,0:T(8,128)S(1)} %fusion.6.depth_ref, f32[2,2,80,2048]{3,2,1,0:T(8,128)S(1)} %branch_1_fun.2.wind_ref), custom_call_target="tpu_custom_call" | custom-call | flops 49152000 | bytes 7864320 | tf_op jit(solution)/shard_map/cond/branch_1_fun/pallas_call | solution.py:209
  43.2 1.1 %copy-done.2 = f32[1,3,64,2048]{3,2,1,0:T(8,128)} copy-done((f32[1,3,64,2048]{3,2,1,0:T(8,128)}, f32[1,3,64,2048]{3,2,1,0:T(8,128)S(1)}, u32[]{:S(2)}) %copy-start.2) | copy-done | bytes 1572888
  (73 shorter events, 5.4 us)
Async XLA Ops:
  3.8 1.9 %collective-permute-start = (f16[3,32,2048]{2,1,0:T(8,128)(2,1)S(1)}, f16[3,32,2048]{2,1,0:T(8,128)(2,1)S(1)}, u32[]{:S(2)}, u32[]{:S(2)}) collective-permute-start(f16[3,32,2048]{2,1,0:T(8,128)(2,1)S(1)} %get-tuple-element.42), channel_id=1, source_target_pairs={{0,2},{2,0},{4,6},{6,4},{8,10},{10,8},{12,14},{14,12},{16,18},{18,... | collective-permute-start | bytes 1179656 | tf_op jit(solution)/shard_map/cond/branch_1_fun/ppermute | solution.py:262
  5.3 5.1 %copy-start.3 = (s32[16]{0:T(128)S(1)}, s32[16]{0:T(128)}, u32[]{:S(2)}) copy-start(s32[16]{0:T(128)} %get-tuple-element.46) | copy-start | bytes 196 | tf_op jit(solution)/shard_map/cond
  5.3 5.9 %copy-start.1 = (f32[64,2048]{1,0:T(8,128)S(1)}, f32[64,2048]{1,0:T(8,128)}, u32[]{:S(2)}) copy-start(f32[64,2048]{1,0:T(8,128)} %get-tuple-element.49) | copy-start | bytes 1572868 | tf_op jit(solution)/shard_map/cond
  6.0 8.7 %collective-permute-start.2 = (f16[2,3,16,2048]{3,2,1,0:T(8,128)(2,1)S(1)}, f16[2,3,16,2048]{3,2,1,0:T(8,128)(2,1)S(1)}, u32[]{:S(2)}, u32[]{:S(2)}) collective-permute-start(f16[2,3,16,2048]{3,2,1,0:T(8,128)(2,1)S(1)} %get-tuple-element.47), channel_id=1, source_target_pairs={{0,4},{4,0},{8,12},{12,8},{16,20},{20,16},{24,28},{28,24},{2,10},{... | collective-permute-start | bytes 1179656 | tf_op jit(solution)/shard_map/cond/branch_1_fun/ppermute | solution.py:262
  8.9 7.8 %collective-permute-start.1 = (f16[2,3,16,2048]{3,2,1,0:T(8,128)(2,1)S(1)}, f16[2,3,16,2048]{3,2,1,0:T(8,128)(2,1)S(1)}, u32[]{:S(2)}, u32[]{:S(2)}) collective-permute-start(f16[2,3,16,2048]{3,2,1,0:T(8,128)(2,1)S(1)} %get-tuple-element.47), channel_id=1, source_target_pairs={{10,18},{14,22},{18,10},{22,14},{11,19},{15,23},{19,11},{23,15}} | collective-permute-start | bytes 1179656 | tf_op jit(solution)/shard_map/cond/branch_1_fun/ppermute | solution.py:262
  9.6 9.3 %collective-permute-start.7 = (f16[2,3,16,2048]{3,2,1,0:T(8,128)(2,1)S(1)}, f16[2,3,16,2048]{3,2,1,0:T(8,128)(2,1)S(1)}, u32[]{:S(2)}, u32[]{:S(2)}) collective-permute-start(f16[2,3,16,2048]{3,2,1,0:T(8,128)(2,1)S(1)} %get-tuple-element.48), channel_id=1, source_target_pairs={{0,4},{4,0},{8,12},{12,8},{16,20},{20,16},{24,28},{28,24},{2,10},{... | collective-permute-start | bytes 1179656 | tf_op jit(solution)/shard_map/cond/branch_1_fun/ppermute | solution.py:262
  9.7 13.1 %collective-permute-start.6 = (f16[2,3,16,2048]{3,2,1,0:T(8,128)(2,1)S(1)}, f16[2,3,16,2048]{3,2,1,0:T(8,128)(2,1)S(1)}, u32[]{:S(2)}, u32[]{:S(2)}) collective-permute-start(f16[2,3,16,2048]{3,2,1,0:T(8,128)(2,1)S(1)} %get-tuple-element.48), channel_id=1, source_target_pairs={{10,18},{14,22},{18,10},{22,14},{11,19},{15,23},{19,11},{23,15}} | collective-permute-start | bytes 1179656 | tf_op jit(solution)/shard_map/cond/branch_1_fun/ppermute | solution.py:262
  11.2 13.1 %collective-permute-start.10 = (f32[3,2048]{1,0:T(4,128)S(1)}, f32[3,2048]{1,0:T(4,128)S(1)}, u32[]{:S(2)}, u32[]{:S(2)}) collective-permute-start(f32[3,2048]{1,0:T(4,128)S(1)} %slice_select_fusion.3), channel_id=1, source_target_pairs={{0,1},{1,0},{2,3},{3,2},{4,5},{5,4},{6,7},{7,6},{8,9},{9,8},{10,11... | collective-permute-start | bytes 73736 | tf_op jit(solution)/shard_map/cond/branch_1_fun/ppermute | solution.py:44
  14.7 9.5 %collective-permute-start.11 = (bf16[80,1024]{1,0:T(8,128)(2,1)S(1)}, bf16[80,1024]{1,0:T(8,128)(2,1)S(1)}, u32[]{:S(2)}, u32[]{:S(2)}) collective-permute-start(bf16[80,1024]{1,0:T(8,128)(2,1)S(1)} %bitcast.142), channel_id=1, source_target_pairs={{0,1},{1,0},{2,3},{3,2},{4,5},{5,4},{6,7},{7,6},{8,9},{9,8},{10,11... | collective-permute-start | bytes 491528 | tf_op jit(solution)/shard_map/cond/branch_1_fun/ppermute | solution.py:72
  17.3 12.1 %collective-permute-start.3 = (f16[2,3,16,2048]{3,2,1,0:T(8,128)(2,1)S(1)}, f16[2,3,16,2048]{3,2,1,0:T(8,128)(2,1)S(1)}, u32[]{:S(2)}, u32[]{:S(2)}) collective-permute-start(f16[2,3,16,2048]{3,2,1,0:T(8,128)(2,1)S(1)} %get-tuple-element.81), channel_id=1, source_target_pairs={{8,16},{12,20},{16,8},{20,12},{9,17},{13,21},{17,9},{21,13}} | collective-permute-start | bytes 1179656 | tf_op jit(solution)/shard_map/cond/branch_1_fun/ppermute | solution.py:262
  18.9 10.5 %collective-permute-start.4 = (f16[2,3,16,2048]{3,2,1,0:T(8,128)(2,1)S(1)}, f16[2,3,16,2048]{3,2,1,0:T(8,128)(2,1)S(1)}, u32[]{:S(2)}, u32[]{:S(2)}) collective-permute-start(f16[2,3,16,2048]{3,2,1,0:T(8,128)(2,1)S(1)} %get-tuple-element.82), channel_id=1, source_target_pairs={{0,8},{4,12},{16,24},{20,28},{8,0},{12,4},{24,16},{28,20},{2,6},{6... | collective-permute-start | bytes 1179656 | tf_op jit(solution)/shard_map/cond/branch_1_fun/ppermute | solution.py:262
  23.5 9.4 %collective-permute-start.9 = (f16[2,3,16,2048]{3,2,1,0:T(8,128)(2,1)S(1)}, f16[2,3,16,2048]{3,2,1,0:T(8,128)(2,1)S(1)}, u32[]{:S(2)}, u32[]{:S(2)}) collective-permute-start(f16[2,3,16,2048]{3,2,1,0:T(8,128)(2,1)S(1)} %get-tuple-element.79), channel_id=1, source_target_pairs={{8,16},{12,20},{16,8},{20,12},{9,17},{13,21},{17,9},{21,13}} | collective-permute-start | bytes 1179656 | tf_op jit(solution)/shard_map/cond/branch_1_fun/ppermute | solution.py:262
  24.2 2.9 %collective-permute-start.12 = (bf16[80,1024]{1,0:T(8,128)(2,1)S(1)}, bf16[80,1024]{1,0:T(8,128)(2,1)S(1)}, u32[]{:S(2)}, u32[]{:S(2)}) collective-permute-start(bf16[80,1024]{1,0:T(8,128)(2,1)S(1)} %fusion.25), channel_id=1, source_target_pairs={{0,2},{2,0},{4,6},{6,4},{8,10},{10,8},{12,14},{14,12},{16,18},{18,... | collective-permute-start | bytes 491528 | tf_op jit(solution)/shard_map/cond/branch_1_fun/ppermute | solution.py:90
  24.3 8.5 %collective-permute-start.8 = (f16[2,3,16,2048]{3,2,1,0:T(8,128)(2,1)S(1)}, f16[2,3,16,2048]{3,2,1,0:T(8,128)(2,1)S(1)}, u32[]{:S(2)}, u32[]{:S(2)}) collective-permute-start(f16[2,3,16,2048]{3,2,1,0:T(8,128)(2,1)S(1)} %get-tuple-element.80), channel_id=1, source_target_pairs={{0,8},{4,12},{16,24},{20,28},{8,0},{12,4},{24,16},{28,20},{2,6},{6... | collective-permute-start | bytes 1179656 | tf_op jit(solution)/shard_map/cond/branch_1_fun/ppermute | solution.py:262
  30.0 3.5 %collective-permute-start.5 = (f16[3,16,2048]{2,1,0:T(8,128)(2,1)S(1)}, f16[3,16,2048]{2,1,0:T(8,128)(2,1)S(1)}, u32[]{:S(2)}, u32[]{:S(2)}) collective-permute-start(f16[3,16,2048]{2,1,0:T(8,128)(2,1)S(1)} %slice_bitcast_fusion.7), channel_id=1, source_target_pairs={{0,2},{2,0},{4,6},{6,4},{8,10},{10,8},{12,14},{14,12},{16,18},{18,... | collective-permute-start | bytes 589832 | tf_op jit(solution)/shard_map/cond/branch_1_fun/ppermute | solution.py:262
  33.4 1.5 %collective-permute-start.13 = (f16[3,16,2048]{2,1,0:T(8,128)(2,1)S(1)}, f16[3,16,2048]{2,1,0:T(8,128)(2,1)S(1)}, u32[]{:S(2)}, u32[]{:S(2)}) collective-permute-start(f16[3,16,2048]{2,1,0:T(8,128)(2,1)S(1)} %slice_bitcast_fusion), channel_id=1, source_target_pairs={{0,2},{2,0},{4,6},{6,4},{8,10},{10,8},{12,14},{14,12},{16,18},{18,... | collective-permute-start | bytes 589832 | tf_op jit(solution)/shard_map/cond/branch_1_fun/ppermute | solution.py:262
  35.1 4.2 %collective-permute-start.14 = (f16[3,3,2048]{2,1,0:T(4,128)(2,1)S(1)}, f16[3,3,2048]{2,1,0:T(4,128)(2,1)S(1)}, u32[]{:S(2)}, u32[]{:S(2)}) collective-permute-start(f16[3,3,2048]{2,1,0:T(4,128)(2,1)S(1)} %slice_select_fusion.2), channel_id=1, source_target_pairs={{0,1},{1,0},{2,3},{3,2},{4,5},{5,4},{6,7},{7,6},{8,9},{9,8},{10,11... | collective-permute-start | bytes 110600 | tf_op jit(solution)/shard_map/cond/branch_1_fun/ppermute | solution.py:44
  43.2 1.1 %copy-start.2 = (f32[1,3,64,2048]{3,2,1,0:T(8,128)}, f32[1,3,64,2048]{3,2,1,0:T(8,128)S(1)}, u32[]{:S(2)}) copy-start(f32[1,3,64,2048]{3,2,1,0:T(8,128)S(1)} %get-tuple-element.167) | copy-start | bytes 4718596
